TPU v7x, 256 devices: a whole 4x4x8 slice. The times are simulated.
256 devices in a mesh: dp: 16 (over x, y_hi, core), etp: 16 (over z, y_lo).
Axes of the slice: x: 4, y: 4 (y_hi: 2, y_lo: 2; y = y_hi * 2 + y_lo), z: 8, core: 2. Of those that a mesh axis runs over, the one named last changes fastest.
Arguments:
- tokens: bfloat16 [32768, 3072], P(('dp', 'etp')), may hold values from -24 to 24
- out_grad: bfloat16 [32768, 3072], P(('dp', 'etp')), may hold values from -4 to 4
- route_ids: int32 [32768, 2], P(('dp', 'etp')), may hold values from 0 to 7, as said below
- route_prob: bfloat16 [32768], P(('dp', 'etp')), may hold values from 0.19921875 to 1
- w_gate: bfloat16 [3072, 8192], P(None, 'etp'), may hold values from -0.109375 to 0.109375
- w_up: bfloat16 [3072, 8192], P(None, 'etp'), may hold values from -0.109375 to 0.109375
- w_down: bfloat16 [8192, 3072], P('etp'), may hold values from -0.0625 to 0.0625
Outputs:
- grad_tokens: bfloat16 [32768, 3072], P(('dp', 'etp'))
- grad_prob: float32 [32768], P(('dp', 'etp'))
- grad_gate: bfloat16 [3072, 8192], P('dp', 'etp')
- grad_up: bfloat16 [3072, 8192], P('dp', 'etp')
- grad_down: bfloat16 [8192, 3072], P('etp', 'dp')
Inputs may be any that keep to these rules, and one draw needn't show every extreme that they name: `route_ids`: each row names two different experts. In each aligned block of 128 rows (the rows of one device) between 24 and 32 rows name expert 0, and in some block exactly 32 rows do.
All inputs are finite; a program needn't handle non-finite values.
Results may differ from a plain program's by a relative error of at most 0.023.
Values may be sent and summed in bfloat16 or wider, within the bound.
A program may use at most 128 MiB of HBM per device.

v0:
```python
import jax
import jax.numpy as jnp
from jax import lax
from jax.sharding import PartitionSpec as P

LOC_CAP = 32


def contract_rows(left, right):
    return lax.dot_general(
        left, right, (((0,), (0,)), ((), ())), preferred_element_type=jnp.float32
    )


def contract_cols(left, right):
    return lax.dot_general(
        left, right, (((1,), (1,)), ((), ())), preferred_element_type=jnp.float32
    )


def shards(tokens, out_grad, route_ids, route_prob, w_gate, w_up, w_down):
    tok_rows = tokens.shape[0]
    hidden_width = w_gate.shape[1]
    data_ways = lax.axis_size("dp")
    routed = jnp.logical_or(route_ids[:, 0] == 0, route_ids[:, 1] == 0)
    positions = jnp.arange(tok_rows, dtype=jnp.int32)
    sort_keys = jnp.where(routed, positions, positions + tok_rows)
    packed_order = jnp.argsort(sort_keys)[:LOC_CAP]
    matches = packed_order[:, None] == positions[None, :]
    selector = matches.astype(jnp.bfloat16)
    x_pack = jnp.dot(selector, tokens, preferred_element_type=jnp.float32).astype(jnp.bfloat16)
    dy_pack = jnp.dot(selector, out_grad, preferred_element_type=jnp.float32).astype(jnp.bfloat16)
    row_weight = jnp.where(routed, route_prob, jnp.zeros_like(route_prob))
    w_pack = row_weight[packed_order]
    x_all, dy_all, w_all = (
        lax.all_gather(x_pack, "etp", axis=0, tiled=True),
        lax.all_gather(dy_pack, "etp", axis=0, tiled=True),
        lax.all_gather(w_pack, "etp", axis=0, tiled=True),
    )
    gate_pre = jnp.dot(x_all, w_gate, preferred_element_type=jnp.float32)
    up_pre = jnp.dot(x_all, w_up, preferred_element_type=jnp.float32)
    sig_gate = jax.nn.sigmoid(gate_pre)
    act_gate = gate_pre * sig_gate
    hidden = (act_gate * up_pre).astype(jnp.bfloat16)
    row_scale = w_all.astype(jnp.float32)[:, None]
    scaled = (row_scale * hidden.astype(jnp.float32)).astype(jnp.bfloat16)
    hidden_raw = contract_cols(dy_all, w_down)
    expert_out = jnp.dot(hidden, w_down, preferred_element_type=jnp.float32)
    prob_part = jnp.sum(expert_out * dy_all.astype(jnp.float32), axis=1)
    prob_share = lax.psum_scatter(prob_part, "etp", scatter_dimension=0, tiled=True)
    grad_hidden = row_scale * hidden_raw
    grad_gate_pre = (grad_hidden * up_pre * sig_gate * (1.0 + gate_pre * (1.0 - sig_gate))).astype(
        jnp.bfloat16
    )
    grad_up_pre = (grad_hidden * act_gate).astype(jnp.bfloat16)
    token_share = lax.psum_scatter(
        (contract_cols(grad_gate_pre, w_gate) + contract_cols(grad_up_pre, w_up)).astype(
            jnp.bfloat16
        ),
        "etp",
        scatter_dimension=0,
        tiled=True,
    )
    grad_tokens = contract_rows(selector, token_share).astype(jnp.bfloat16)
    spread_prob = jnp.where(matches, prob_share[:, None], jnp.zeros_like(prob_share)[:, None])
    grad_prob = jnp.sum(spread_prob, axis=0) * routed.astype(jnp.float32)
    gate_up = jnp.concatenate([grad_gate_pre, grad_up_pre], axis=1)
    shares = lax.psum_scatter(
        jnp.concatenate(
            [contract_rows(x_all, gate_up), contract_rows(dy_all, scaled)], axis=1
        ).astype(jnp.bfloat16),
        "dp",
        scatter_dimension=0,
        tiled=True,
    ).astype(jnp.float32)
    shares = shares / data_ways
    grad_gate = shares[:, :hidden_width].astype(jnp.bfloat16)
    grad_up = shares[:, hidden_width : 2 * hidden_width].astype(jnp.bfloat16)
    grad_down = jnp.transpose(shares[:, 2 * hidden_width :]).astype(jnp.bfloat16)
    return (grad_tokens, grad_prob, grad_gate, grad_up, grad_down)


def solution(mesh):
    placed = (
        P(("dp", "etp"), None),
        P(("dp", "etp"), None),
        P(("dp", "etp"), None),
        P(("dp", "etp")),
        P(None, "etp"),
        P(None, "etp"),
        P("etp", None),
    )
    return jax.shard_map(
        shards,
        mesh=mesh,
        in_specs=placed,
        out_specs=(
            P(("dp", "etp"), None),
            P(("dp", "etp")),
            P("dp", "etp"),
            P("dp", "etp"),
            P("etp", "dp"),
        ),
        check_vma=False,
    )
```

profile of v0, /device:TPU:1, one launch (start us, length us, event | category | flops | bytes accessed | tf_op | source)
XLA Modules:
  0.0 409.6 jit_solution(1921893589972458012)
XLA Ops:
  8.1 2.5 sort.17
  10.7 2.1 convolution_convert_fusion.3
  12.8 2.1 convolution_convert_fusion.4
  15.7 1.3 fusion.9
  18.0 32.6 %all-reduce = bf16[512]{0:T(512)(128)(2,1)S(1)} all-reduce(bf16[512]{0:T(512)(128)(2,1)S(1)} %dynamic-update-slice), channel_id=2, replica_groups=mesh['dp'=16,'etp'=16] {'etp'}, use_global_device_ids=true, to_apply=%add | all-reduce | flops 512 | bytes 2048
  50.6 44.6 %all-gather.6.cloned.1.call-done = bf16[512,3072]{1,0:T(8,128)(2,1)} async-done(((bf16[32,3072]{1,0:T(8,128)(2,1)}), bf16[512,3072]{1,0:T(8,128)(2,1)}) %all-gather.6.cloned.1.call-update) | async-done | bytes 3145744 | tf_op jit(solution)/shard_map/all_gather | solution.py:36
  95.2 5.7 %fusion.10 = f32[512,512]{0,1:T(8,128)} fusion(bf16[512,3072]{1,0:T(8,128)(2,1)} %all-gather.6.cloned.1.call-done, bf16[3072,512]{1,0:T(8,128)(2,1)} %param.11), kind=kOutput, calls=%fused_computation.35 | convolution fusion | flops 1610612736 | bytes 7340032 | tf_op jit(solution)/shard_map/dot_general | solution.py:40
  100.8 78.1 %all-gather.4.cloned.1.call-done = bf16[512,3072]{1,0:T(8,128)(2,1)} async-done(((bf16[32,3072]{1,0:T(8,128)(2,1)}), bf16[512,3072]{1,0:T(8,128)(2,1)}) %all-gather.4.cloned.1.call-update) | async-done | bytes 3145744 | tf_op jit(solution)/shard_map/all_gather | solution.py:37
  178.9 4.8 %convolution_multiply_fusion = f32[512,512]{0,1:T(8,128)S(1)} fusion(bf16[512,3072]{1,0:T(8,128)(2,1)} %all-gather.4.cloned.1.call-done, bf16[512,3072]{1,0:T(8,128)(2,1)} %param.13, f32[512]{0:T(512)S(1)} %convert_element_type.45), kind=kOutput, calls=%fused_computation.10 | convolution fusion | flops 1610874880 | bytes 7342080 | tf_op jit(solution)/shard_map/dot_general | solution.py:16
  183.8 3.0 multiply_convert_fusion.2
  186.8 1.9 fusion.11
  188.7 3.6 add_convert_fusion
  192.6 4.0 convolution_convert_fusion.1
  196.6 4.4 %convolution_convert_fusion = bf16[3072,1024]{0,1:T(8,128)(2,1)S(1)} fusion(bf16[512,3072]{1,0:T(8,128)(2,1)S(1)} %copy-done.7, bf16[512,512]{0,1:T(8,128)(2,1)S(1)} %copy-done.5, bf16[512,512]{0,1:T(8,128)(2,1)S(1)} %copy-done.3), kind=kOutput, calls=%fused_computation.4 | convolution fusion | flops 3226468352 | bytes 10485760 | tf_op jit(solution)/shard_map/dot_general | solution.py:10
  201.0 4.5 %pad_maximum_fusion = bf16[3072,1536]{0,1:T(8,128)(2,1)} fusion(bf16[3072,512]{0,1:T(8,128)(2,1)S(1)} %convolution_convert_fusion.1, bf16[3072,1024]{0,1:T(8,128)(2,1)S(1)} %convolution_convert_fusion), kind=kLoop, calls=%fused_computation.1 | loop fusion | flops 18874368 | bytes 18874368 | tf_op jit(solution)/shard_map/concatenate | solution.py:69
  205.5 12.7 %copy.24 = bf16[3072,1536]{1,0:T(8,128)(2,1)} copy(bf16[3072,1536]{0,1:T(8,128)(2,1)} %pad_maximum_fusion) | data formatting | bytes 18874368
  218.9 5.0 %multiply_reduce_fusion = f32[512]{0:T(512)S(1)} fusion(bf16[512,3072]{1,0:T(8,128)(2,1)} %all-gather.4.cloned.1.call-done, bf16[512,512]{0,1:T(8,128)(2,1)} %get-tuple-element.29, bf16[512,3072]{1,0:T(8,128)(2,1)} %param.13), kind=kOutput, calls=%fused_computation.2 | convolution fusion | flops 1615330816 | bytes 6817792 | tf_op jit(solution)/shard_map/dot_general | solution.py:48
  224.0 27.6 %all-reduce.1 = f32[512]{0:T(512)S(1)} all-reduce(f32[512]{0:T(512)S(1)} %multiply_reduce_fusion), channel_id=4, replica_groups=mesh['dp'=16,'etp'=16] {'etp'}, use_global_device_ids=true, to_apply=%region_3.4.clone | all-reduce | flops 512 | bytes 4096
  252.3 21.1 %reduce-scatter.5.cloned.1.call-done = bf16[32,3072]{1,0:T(8,128)(2,1)} async-done(((bf16[512,3072]{1,0:T(8,128)(2,1)}), bf16[32,3072]{1,0:T(8,128)(2,1)}) %reduce-scatter.5.cloned.1.call-update) | async-done | bytes 196624 | tf_op jit(solution)/shard_map/reduce_scatter | solution.py:56
  273.4 2.3 convolution_convert_fusion.2
  275.7 118.7 %reduce-scatter.7.cloned.1.call-done = bf16[192,1536]{1,0:T(8,128)(2,1)} async-done(((bf16[3072,1536]{1,0:T(8,128)(2,1)}), bf16[192,1536]{1,0:T(8,128)(2,1)}) %reduce-scatter.7.cloned.1.call-update) | async-done | bytes 589840
  394.4 2.2 copy.25
  398.7 1.8 copy.21
  400.5 1.8 copy.22
  (41 shorter events, 5.9 us)
Async XLA Ops:
  7.2 176.6 %copy-start = (bf16[3072,512]{1,0:T(8,128)(2,1)S(1)}, bf16[3072,512]{1,0:T(8,128)(2,1)}, u32[]{:S(2)}) copy-start(bf16[3072,512]{1,0:T(8,128)(2,1)} %param.12) | copy-start | bytes 9437188
  7.2 88.0 %all-gather.6.cloned.1.call-start = ((), (), s32[]{:S(2)}) async-start(), calls=%async_computation.3 | async-start | bytes 3342336 | tf_op jit(solution)/shard_map/all_gather | solution.py:36
  12.8 166.2 %all-gather.4.cloned.1.call-start = ((), (), s32[]{:S(2)}) async-start(), calls=%async_computation.2 | async-start | bytes 3342336 | tf_op jit(solution)/shard_map/all_gather | solution.py:37
  14.9 258.5 %reduce-scatter.5.cloned.1.call-start = ((), (), s32[]{:S(2)}) async-start(), calls=%async_computation.4 | async-start | bytes 3342336 | tf_op jit(solution)/shard_map/reduce_scatter | solution.py:56
  178.9 4.8 %copy-start.6 = (bf16[512,3072]{1,0:T(8,128)(2,1)S(1)}, bf16[512,3072]{1,0:T(8,128)(2,1)}, u32[]{:S(2)}) copy-start(bf16[512,3072]{1,0:T(8,128)(2,1)} %all-gather.6.cloned.1.call-done) | copy-start | bytes 9437188
  178.9 4.8 %copy-start.8 = (f32[512,512]{0,1:T(8,128)S(1)}, f32[512,512]{0,1:T(8,128)}, u32[]{:S(2)}) copy-start(f32[512,512]{0,1:T(8,128)} %fusion.10) | copy-start | bytes 3145732
  183.8 3.1 copy-start.1
  186.8 1.9 copy-start.2
  186.8 1.9 copy-start.4
  192.3 202.1 %reduce-scatter.7.cloned.1.call-start = ((), (), s32[]{:S(2)}) async-start(), calls=%async_computation.5 | async-start | bytes 10027008
  192.6 4.0 copy-start.3
  192.6 4.0 copy-start.5
  192.6 4.0 copy-start.7
Sparse Core Ops, SparseCore 0:
  12.9 82.2 all-gather.5
  97.5 81.3 all-gather.3
  192.5 80.9 reduce-scatter.4
  278.0 116.3 reduce-scatter.6
where the time goes:
time: 410 us
  waiting for transfers between devices  263 us (64%)
  blocking collectives  60.2 us (15%)
  matrix products  38.9 us (9%)
  local copies, waits for them, and re-layouts  22.5 us (5%)
  between operations  15.3 us (4%)
  other arithmetic  9.82 us (2%)
    unnamed x5, waiting for transfers between devices  119 us
    all_gather x1, waiting for transfers between devices, shards(): lax.all_gather(dy_pack, 'etp', axis=0, tiled=True)  78.1 us
    unnamed x2, blocking collectives  60.2 us
    all_gather x1, waiting for transfers between devices, shards(): lax.all_gather(x_pack, 'etp', axis=0, tiled=True)  44.6 us
    reduce_scatter x1, waiting for transfers between devices, shards(): lax.psum_scatter((contract_cols(grad_gate_pre, w_gate) + contract_cols(gr...  21.1 us
    unnamed x27, local copies, waits for them, and re-layouts  21 us
    dot_general x3, matrix products, contract_rows(): lax.dot_general(left, right, (((0,), (0,)), ((), ())), preferred_element_...  10.7 us
    dot_general x3, matrix products, contract_cols(): lax.dot_general(left, right, (((1,), (1,)), ((), ())), preferred_element_...  10.3 us
  transfers between devices with their start and end apart: 4, of which 4 were waited for; matrix products, arithmetic and copies ran while one was open for 11% of the time, Pallas kernels for 0%

commit v1 on v0

v1 whole, which is shorter than its diff:
```python
import functools

import jax
import jax.numpy as jnp
from jax import lax
from jax.experimental import pallas as pl
from jax.experimental.pallas import tpu as pltpu
from jax.sharding import PartitionSpec as P

MESH = pl.DeviceIdType.MESH
CAP = 32
BF = jnp.bfloat16
F32 = jnp.float32

ORDER = (
    (0, 0), (1, 0), (0, 1), (0, -1),
    (0, 2), (0, -2), (1, 1), (1, -1),
    (0, 3), (0, -3), (0, 4), (1, 2),
    (1, -2), (1, 3), (1, -3), (1, 4),
)
SLOT = {key: i for i, key in enumerate(ORDER)}
CHUNKS = ((2, 1), (2, 0), (1, 1), (-1, 1), (1, 0), (-1, 0), (0, 1), (0, 0))
CIDX = {key: i for i, key in enumerate(CHUNKS)}


def pair_row(col, off):
    return ((off % 8) * 2 + col) * CAP


def dot(a, b):
    return jnp.dot(a, b, preferred_element_type=F32)


def dot_t(a, b):
    return lax.dot_general(a, b, (((1,), (1,)), ((), ())), preferred_element_type=F32)


def kernel(
    ids, prob, tokens, out_grad, w_gate_h, w_up_h, w_down_h,
    o_tok, o_prob, o_w,
    wg, wu, wd, xs, ds, xt, dt, gs, tp, pb, ws, sr, xa, xb, yb, rp, rph, pr, ry, pry,
    w_sem, s_sem, r_sem,
):
    D = tokens.shape[1]
    F = wg.shape[1]
    H = D // 2
    rows_own = o_w.shape[1]
    half = rows_own // 2
    dp, etp = lax.axis_index("dp"), lax.axis_index("etp")
    x, yh, core = dp // 4, (dp // 2) % 2, dp % 2
    z, yl = etp // 2, etp % 2

    def dp_of(px, ph, pc):
        return px * 4 + ph * 2 + pc

    dev = {
        "z+": (dp, ((z + 1) % 8) * 2 + yl),
        "z-": (dp, ((z + 7) % 8) * 2 + yl),
        "yl": (dp, z * 2 + 1 - yl),
        "x+": (dp_of((x + 1) % 4, yh, core), etp),
        "x-": (dp_of((x + 3) % 4, yh, core), etp),
        "y2": (dp_of(x, 1 - yh, core), etp),
        "c": (dp_of(x, yh, 1 - core), etp),
    }

    loads = []
    for i, (src, dst) in enumerate(((w_gate_h, wg), (w_up_h, wu), (w_down_h, wd))):
        cp = pltpu.make_async_copy(src, dst, w_sem.at[i])
        cp.start()
        loads.append(cp)

    barrier = pltpu.get_barrier_semaphore()
    for name in dev:
        pl.semaphore_signal(barrier, inc=1, device_id=dev[name], device_id_type=MESH)

    count = [0]
    sent = []

    def send(name, src, dst):
        i = count[0]
        count[0] += 1
        cp = pltpu.make_async_remote_copy(
            src_ref=src, dst_ref=dst, send_sem=s_sem.at[i], recv_sem=r_sem.at[i],
            device_id=dev[name], device_id_type=MESH,
        )
        cp.start()
        sent.append(cp)
        return cp

    routed = jnp.logical_or(ids[0:1, :] == 0, ids[1:2, :] == 0)
    n_tok = routed.shape[1]
    routed_f = jnp.where(routed, 1.0, 0.0).astype(F32)
    before = (
        lax.broadcasted_iota(jnp.int32, (n_tok, n_tok), 0)
        < lax.broadcasted_iota(jnp.int32, (n_tok, n_tok), 1)
    )
    rank = dot(
        jnp.broadcast_to(routed_f, (16, n_tok)).astype(BF),
        jnp.where(before, 1.0, 0.0).astype(BF),
    )[0:1, :]
    slot_no = lax.broadcasted_iota(jnp.int32, (CAP, n_tok), 0).astype(F32)
    sel = jnp.where(
        jnp.logical_and(
            jnp.broadcast_to(rank, (CAP, n_tok)) == slot_no,
            jnp.broadcast_to(routed_f, (CAP, n_tok)) > 0.5,
        ),
        1.0,
        0.0,
    ).astype(F32)
    sel_b = sel.astype(BF)
    xs[0:CAP, :] = dot(sel_b, tokens[...]).astype(BF)
    ds[0:CAP, 0:D] = dot(sel_b, out_grad[...]).astype(BF)
    w_own = jnp.sum(sel * prob[...].astype(F32), axis=1, keepdims=True)
    ds[0:CAP, D:] = jnp.broadcast_to(w_own, (CAP, 128)).astype(BF)

    pl.semaphore_wait(barrier, len(dev))

    arriving = {}

    def gsend(name, key, to, parts="xd"):
        a, b = pl.ds(SLOT[key] * CAP, CAP), pl.ds(SLOT[to] * CAP, CAP)
        for part in parts:
            buf = xs if part == "x" else ds
            arriving[to + (part,)] = send(name, buf.at[a, :], buf.at[b, :])

    def gwait(*keys, parts="xd"):
        for key in keys:
            for part in parts:
                arriving[key + (part,)].wait_recv()

    def compute(g):
        rows = slice(g * 128, (g + 1) * 128)
        wcol = ds[rows, D:].astype(F32)[:, 0:1]
        n_f = 2
        fw = F // n_f
        psum = jnp.zeros((128, 1), F32)
        for f in range(n_f):
            cols = slice(f * fw, (f + 1) * fw)
            gate = dot(xs[rows, :], wg[:, cols])
            up = dot(xs[rows, :], wu[:, cols])
            raw = dot_t(ds[rows, 0:D], wd[cols, :])
            sig = 1.0 / (1.0 + jnp.exp(-gate))
            act = gate * sig
            hid = (act * up).astype(BF).astype(F32)
            gh = wcol * raw
            gs[2, rows, cols] = (wcol * hid).astype(BF)
            gs[0, rows, cols] = (gh * up * sig * (1.0 + gate * (1.0 - sig))).astype(BF)
            gs[1, rows, cols] = (gh * act).astype(BF)
            psum = psum + jnp.sum(hid * raw, axis=1, keepdims=True)
        pbr = jnp.broadcast_to(psum, (128, 128))
        for q in range(4):
            r = pair_row(*ORDER[4 * g + q])
            pb[r : r + CAP, :] = pbr[q * CAP : (q + 1) * CAP, :]

        def tok_tile(n, carry):
            at = pl.multiple_of(n * 512, 512)
            t = (
                dot_t(gs[0, rows, :], wg[pl.ds(at, 512), :])
                + dot_t(gs[1, rows, :], wu[pl.ds(at, 512), :])
            ).astype(BF)
            for q in range(4):
                r = pair_row(*ORDER[4 * g + q])
                tp[r : r + CAP, pl.ds(at, 512)] = t[q * CAP : (q + 1) * CAP, :]
            return carry

        lax.fori_loop(0, D // 512, tok_tile, 0)

        def turn(n, carry):
            at = pl.multiple_of(n * 256, 256)
            xt[pl.ds(at, 256), rows] = xs[rows, pl.ds(at, 256)].T
            dt[pl.ds(at, 256), rows] = ds[rows, pl.ds(at, 256)].T
            return carry

        lax.fori_loop(0, D // 256, turn, 0)

    for name in ("z+", "z-", "yl"):
        gsend(name, (0, 0), {"z+": (0, 1), "z-": (0, -1), "yl": (1, 0)}[name])
    for cp in loads:
        cp.wait()
    gwait((0, 1))
    gsend("z+", (0, 1), (0, 2))
    gwait((0, -1))
    gsend("z-", (0, -1), (0, -2))
    gwait((1, 0))
    gsend("yl", (0, 1), (1, 1))
    gsend("yl", (0, -1), (1, -1))
    compute(0)
    gwait((0, 2))
    gsend("z+", (0, 2), (0, 3))
    gwait((0, -2))
    gsend("z-", (0, -2), (0, -3))
    gwait((1, 1), (1, -1))
    gsend("yl", (0, 2), (1, 2), "x")
    gsend("yl", (0, -2), (1, -2), "x")
    gwait((0, 3))
    gsend("z+", (0, 3), (0, 4), "x")
    gsend("z+", (1, 1), (1, 2), "d")
    gwait((0, -3))
    gsend("z-", (0, -3), (0, 4), "d")
    gsend("z-", (1, -1), (1, -2), "d")
    compute(1)
    gwait((0, 4))
    gsend("yl", (0, 4), (1, 4))
    gwait((1, 2))
    gsend("z+", (1, 2), (1, 3))
    gwait((1, -2))
    gsend("z-", (1, -2), (1, -3))
    compute(2)
    gwait((1, 3), (1, -3), (1, 4))
    compute(3)

    def add_rows(dst, dst_row, src, src_row, n, cols):
        def body(i, carry):
            a = pl.ds(pl.multiple_of(dst_row + i * 16, 16), 16)
            b = pl.ds(pl.multiple_of(src_row + i * 16, 16), 16)
            dst[a, cols] = (dst[a, cols].astype(F32) + src[b, :].astype(F32)).astype(BF)
            return carry

        lax.fori_loop(0, n // 16, body, 0)

    chain = {"z+": {}, "z-": {}}
    PAIR = 2 * CAP
    side = {"z+": 0, "z-": 1}

    def tok_step(k):
        for name, sign in (("z+", -1), ("z-", 1)):
            i = side[name]
            r = pair_row(0, sign * k)
            if k == 4:
                cols = slice(0, H) if i == 0 else slice(H, D)
                got = send(name, tp.at[pl.ds(r, PAIR), cols], rph.at[i])
                gotp = None
                if i == 0:
                    gotp = send(name, pb.at[pl.ds(r, PAIR), :], pr.at[i, 0])
            else:
                before_t, before_p = chain[name][k + 1]
                before_t.wait_recv()
                if k == 3:
                    cols = slice(0, H) if i == 0 else slice(H, D)
                    add_rows(tp, r, rph.at[i], 0, PAIR, cols)
                else:
                    add_rows(tp, r, rp.at[i, 2 - k], 0, PAIR, slice(0, D))
                if before_p is not None:
                    before_p.wait_recv()
                    pb[r : r + PAIR, :] = pb[r : r + PAIR, :] + pr[i, 3 - k]
                got = send(name, tp.at[pl.ds(r, PAIR), :], rp.at[i, 3 - k])
                gotp = send(name, pb.at[pl.ds(r, PAIR), :], pr.at[i, 4 - k])
            chain[name][k] = (got, gotp)

    def tok_sum():
        for name in ("z+", "z-"):
            chain[name][1][0].wait_recv()
            chain[name][1][1].wait_recv()
        a = slice(CAP, PAIR)
        tp[a, :] = (
            tp[a, :].astype(F32) + rp[0, 2, a, :].astype(F32) + rp[1, 2, a, :].astype(F32)
        ).astype(BF)
        pb[a, :] = pb[a, :] + pr[0, 3, a, :] + pr[1, 3, a, :]
        t = send("yl", tp.at[pl.ds(CAP, CAP), :], ry)
        p = send("yl", pb.at[pl.ds(CAP, CAP), :], pry)
        return t, p

    def tok_final(t, p):
        t.wait_recv()
        a = slice(0, CAP)
        total = (
            tp[a, :].astype(F32) + rp[0, 2, a, :].astype(F32) + rp[1, 2, a, :].astype(F32)
            + ry[...].astype(F32)
        ).astype(BF)
        o_tok[...] = dot(sel.T.astype(BF), total).astype(BF)
        p.wait_recv()
        psum = pb[a, :] + pr[0, 3, a, :] + pr[1, 3, a, :] + pry[...]
        o_prob[...] = jnp.sum(sel * psum, axis=0, keepdims=True)

    def chunk_dot(key, pc, p):
        dx, h = key
        owner = dp_of((x + dx + 4) % 4, (yh + h) % 2, pc)
        at = pl.multiple_of(owner * rows_own, 64)
        lhs = dt if p == 2 else xt
        return dot(lhs[pl.ds(at, rows_own), :], gs[p])

    tok_step(4)
    from_core = []
    for i, key in enumerate(CHUNKS):
        for p in range(3):
            ws[i, p] = chunk_dot(key, 1 - core, p).astype(BF)
        from_core.append(send("c", ws.at[i], sr.at[i]))

    def own_chunk(key):
        i = CIDX[key]
        from_core[i].wait_recv()
        for p in range(3):
            sr[i, p] = (chunk_dot(key, core, p) + sr[i, p].astype(F32)).astype(BF)

    far = {}

    def far_send(h):
        i = CIDX[(2, h)]
        for s, name in ((0, "x+"), (1, "x-")):
            far[name, h] = send(name, sr.at[i, :, pl.ds(s * half, half), :], xa.at[s, h])

    near = {}

    def near_add(h):
        for s, name, dx in ((0, "x+", 1), (1, "x-", -1)):
            far[name, h].wait_recv()
            i = CIDX[(dx, h)]
            r = slice(s * half, (s + 1) * half)
            for p in range(3):
                sr[i, p, r, :] = (sr[i, p, r, :].astype(F32) + xa[s, h, p].astype(F32)).astype(BF)

    def near_send(h, p):
        for s, name, dx in ((0, "x+", 1), (1, "x-", -1)):
            near[name, h, p] = send(name, sr.at[CIDX[(dx, h)], p], xb.at[s, h, p])

    def near_wait(h, p):
        for name in ("x+", "x-"):
            near[name, h, p].wait_recv()

    to_y = {}

    own_chunk((2, 1))
    far_send(1)
    own_chunk((2, 0))
    far_send(0)
    own_chunk((1, 1))
    own_chunk((-1, 1))
    tok_step(3)
    near_add(1)
    for p in range(3):
        near_send(1, p)
    own_chunk((1, 0))
    own_chunk((-1, 0))
    own_chunk((0, 1))
    own_chunk((0, 0))
    tok_step(2)
    near_add(0)
    tok_step(1)

    def y_send(p):
        near_wait(1, p)
        i = CIDX[(0, 1)]
        sr[i, p] = (
            sr[i, p].astype(F32) + xb[0, 1, p].astype(F32) + xb[1, 1, p].astype(F32)
        ).astype(BF)
        to_y[p] = send("y2", sr.at[i, p], yb.at[p])

    for p in range(3):
        y_send(p)
        near_send(0, p)
    t, q = tok_sum()
    tok_final(t, q)
    i = CIDX[(0, 0)]
    for p in range(3):
        near_wait(0, p)
        to_y[p].wait_recv()
        o_w[p] = (
            (
                sr[i, p].astype(F32) + xb[0, 0, p].astype(F32) + xb[1, 0, p].astype(F32)
                + yb[p].astype(F32)
            )
            * (1.0 / 16.0)
        ).astype(BF)
    for cp in sent:
        cp.wait_send()


def shards(tokens, out_grad, route_ids, route_prob, w_gate, w_up, w_down):
    n_tok, D = tokens.shape
    F = w_gate.shape[1]
    own = D // lax.axis_size("dp")
    rows = CAP * lax.axis_size("etp")
    vmem = pl.BlockSpec(memory_space=pltpu.VMEM)
    hbm = pl.BlockSpec(memory_space=pl.ANY)
    n_sem = 100
    scratch = [
        pltpu.VMEM((D, F), BF),
        pltpu.VMEM((D, F), BF),
        pltpu.VMEM((F, D), BF),
        pltpu.VMEM((rows, D), BF),
        pltpu.VMEM((rows, D + 128), BF),
        pltpu.VMEM((D, rows), BF),
        pltpu.VMEM((D, rows), BF),
        pltpu.VMEM((3, rows, F), BF),
        pltpu.VMEM((rows, D), BF),
        pltpu.VMEM((rows, 128), F32),
        pltpu.VMEM((8, 3, own, F), BF),
        pltpu.VMEM((8, 3, own, F), BF),
        pltpu.VMEM((2, 2, 3, own // 2, F), BF),
        pltpu.VMEM((2, 2, 3, own, F), BF),
        pltpu.VMEM((3, own, F), BF),
        pltpu.VMEM((2, 3, 2 * CAP, D), BF),
        pltpu.VMEM((2, 2 * CAP, D // 2), BF),
        pltpu.VMEM((2, 4, 2 * CAP, 128), F32),
        pltpu.VMEM((CAP, D), BF),
        pltpu.VMEM((CAP, 128), F32),
        pltpu.SemaphoreType.DMA((3,)),
        pltpu.SemaphoreType.DMA((n_sem,)),
        pltpu.SemaphoreType.DMA((n_sem,)),
    ]
    g_tok, g_prob, g_w = pl.pallas_call(
        kernel,
        out_shape=(
            jax.ShapeDtypeStruct((n_tok, D), BF),
            jax.ShapeDtypeStruct((1, n_tok), F32),
            jax.ShapeDtypeStruct((3, own, F), BF),
        ),
        in_specs=[vmem] * 4 + [hbm] * 3,
        out_specs=(vmem, vmem, vmem),
        scratch_shapes=scratch,
        compiler_params=pltpu.CompilerParams(
            collective_id=0, has_side_effects=True, vmem_limit_bytes=60 * 1024 * 1024
        ),
        cost_estimate=pl.CostEstimate(
            flops=8 * 2 * rows * D * F, bytes_accessed=6 * D * F + 8 * n_tok * D, transcendentals=rows * F
        ),
    )(route_ids.T, route_prob.reshape(1, n_tok), tokens, out_grad, w_gate, w_up, w_down)
    return g_tok, g_prob.reshape(n_tok), g_w[0], g_w[1], g_w[2].T


def solution(mesh):
    placed = (
        P(("dp", "etp"), None),
        P(("dp", "etp"), None),
        P(("dp", "etp"), None),
        P(("dp", "etp")),
        P(None, "etp"),
        P(None, "etp"),
        P("etp", None),
    )
    return jax.shard_map(
        shards,
        mesh=mesh,
        in_specs=placed,
        out_specs=(
            P(("dp", "etp"), None),
            P(("dp", "etp")),
            P("dp", "etp"),
            P("dp", "etp"),
            P("etp", "dp"),
        ),
        check_vma=False,
    )
```

time: 410 us -> 116 us (0.28)
  waiting for transfers between devices: 263 us -> 0 us
  Pallas kernels: 0 us -> 108 us
  blocking collectives: 60.2 us -> 0 us
  matrix products: 38.9 us -> 0 us
  local copies, waits for them, and re-layouts: 22.5 us -> 5.08 us
  between operations: 15.3 us -> 0.64 us
  other arithmetic: 9.82 us -> 0 us
    all_gather x2 -> x0, waiting for transfers between devices: 123 us -> none  [the longest x1 78.1 us: shards(): lax.all_gather(dy_pack, 'etp', axis=0, tiled=True)]
    unnamed x5 -> x0, waiting for transfers between devices: 119 us -> none
    pallas_call x0 -> x1, Pallas kernels: none -> 108 us  [shards(): pl.pallas_call(kernel, out_shape=(jax.ShapeDtypeStruct((n_tok, D), BF), j...]
    unnamed x2 -> x0, blocking collectives: 60.2 us -> none
    dot_general x11 -> x0, matrix products: 38.9 us -> none  [the longest x3 10.7 us: contract_rows(): lax.dot_general(left, right, (((0,), (0,)), ((), ())), preferred_element_...]
    reduce_scatter x1 -> x0, waiting for transfers between devices: 21.1 us -> none  [shards(): lax.psum_scatter((contract_cols(grad_gate_pre, w_gate) + contract_cols(gr...]
    unnamed x27 -> x2, local copies, waits for them, and re-layouts: 21 us -> 3.14 us
    concatenate x1 -> x0, other arithmetic: 4.51 us -> none  [shards(): jnp.concatenate([contract_rows(x_all, gate_up), contract_rows(dy_all, sca...]
  transfers between devices with their start and end apart: 4 -> 0, of which waited for: 4 -> 0; matrix products, arithmetic and copies ran while one was open for 11% -> 0% of each run, Pallas kernels for 0% -> 0%
where the time goes in v1:
time: 116 us; the launch traced here: 114 us
  Pallas kernels  108 us (93%)
  local copies, waits for them, and re-layouts  5.08 us (4%)
    pallas_call x1, Pallas kernels, shards(): pl.pallas_call(kernel, out_shape=(jax.ShapeDtypeStruct((n_tok, D), BF), j...  108 us
    unnamed x2, local copies, waits for them, and re-layouts  3.14 us

profile of v1, /device:TPU:1, one launch (start us, length us, event | category | flops | bytes accessed | tf_op | source)
XLA Modules:
  0.0 114.1 jit_solution(17882476604154912757)
XLA Ops:
  0.6 108.3 %shard_map.110 = (bf16[128,3072]{1,0:T(8,128)(2,1)}, f32[1,128]{1,0:T(1,128)}, bf16[3,192,512]{2,1,0:T(8,128)(2,1)}) custom-call(s32[2,128]{1,0:T(2,128)} %bitcast.11, bf16[1,128]{1,0:T(2,128)(2,1)} %bitcast.12, bf16[128,3072]{1,0:T(8,128)(2,1)} %tokens.1, bf16[128,3072]{1,0:T(8,128)(2,1)} %out_grad.1, bf16[3072,512]{1,0:T(8,128)(2,1)} %w_gate_h.1, ...), custom_call_target="tpu_custom_call" | custom-call | flops 12884901888 | bytes 12582912 | tf_op jit(solution)/shard_map/pallas_call | solution.py:401
  109.0 1.9 %slice_bitcast_fusion = (bf16[512,192]{0,1:T(8,128)(2,1)}, bf16[192,512]{1,0:T(8,128)(2,1)}, bf16[192,512]{1,0:T(8,128)(2,1)}) fusion(bf16[3,192,512]{2,1,0:T(8,128)(2,1)} %get-tuple-element.10), kind=kLoop, calls=%fused_computation | loop fusion | bytes 1179648 | tf_op jit(solution)/shard_map/transpose | solution.py:418
  110.9 2.1 %copy.14 = bf16[128,3072]{1,0:T(8,128)(2,1)} copy(bf16[128,3072]{1,0:T(8,128)(2,1)} %get-tuple-element.19) | data formatting | bytes 1572864
  113.0 1.1 copy.15

commit v2 on v1

v2 whole, which is shorter than its diff:
```python
import functools

import jax
import jax.numpy as jnp
from jax import lax
from jax.experimental import pallas as pl
from jax.experimental.pallas import tpu as pltpu
from jax.sharding import PartitionSpec as P

MESH = pl.DeviceIdType.MESH
CAP = 32
BF = jnp.bfloat16
F32 = jnp.float32

ORDER = (
    (0, 0), (1, 0), (0, 1), (0, -1),
    (0, 2), (0, -2), (1, 1), (1, -1),
    (0, 3), (0, -3), (0, 4), (1, 2),
    (1, -2), (1, 3), (1, -3), (1, 4),
)
SLOT = {key: i for i, key in enumerate(ORDER)}
CHUNKS = ((2, 0), (2, 1), (1, 0), (1, 1), (-1, 0), (-1, 1), (0, 0), (0, 1))
CIDX = {key: i for i, key in enumerate(CHUNKS)}


def pair_row(col, off):
    return ((off % 8) * 2 + col) * CAP


def dot(a, b):
    return jnp.dot(a, b, preferred_element_type=F32)


def dot_t(a, b):
    return lax.dot_general(a, b, (((1,), (1,)), ((), ())), preferred_element_type=F32)


def routed_rows(ids):
    routed = jnp.logical_or(ids[0:1, :] == 0, ids[1:2, :] == 0)
    n_tok = routed.shape[1]
    routed_f = jnp.where(routed, 1.0, 0.0).astype(F32)
    before = (
        lax.broadcasted_iota(jnp.int32, (n_tok, n_tok), 0)
        < lax.broadcasted_iota(jnp.int32, (n_tok, n_tok), 1)
    )
    rank = dot(
        jnp.broadcast_to(routed_f, (16, n_tok)).astype(BF),
        jnp.where(before, 1.0, 0.0).astype(BF),
    )[0:1, :]
    slot_no = lax.broadcasted_iota(jnp.int32, (CAP, n_tok), 0).astype(F32)
    chosen = jnp.logical_and(
        jnp.broadcast_to(rank, (CAP, n_tok)) == slot_no,
        jnp.broadcast_to(routed_f, (CAP, n_tok)) > 0.5,
    )
    return jnp.where(chosen, 1.0, 0.0).astype(F32)


def kernel(
    ids, prob, tokens_h, out_grad_h, w_gate_h, w_up_h, w_down_h,
    o_tok, o_prob, o_w,
    tokens, out_grad, wg, wu, wd, wgt, wut, xs, ds, xt, dt, gs, tp, pb, ws, sr, xa, xb, yb, yc,
    rp, rph, pr, ry, pry, fw,
    w_sem, o_sem, s_sem, r_sem,
):
    D = xs.shape[1]
    F = wg.shape[1]
    H = D // 2
    rows_own = fw.shape[1]
    half = rows_own // 2
    dp, etp = lax.axis_index("dp"), lax.axis_index("etp")
    x, yh, core = dp // 4, (dp // 2) % 2, dp % 2
    z, yl = etp // 2, etp % 2

    def dp_of(px, ph, pc):
        return px * 4 + ph * 2 + pc

    dev = {
        "z+": (dp, ((z + 1) % 8) * 2 + yl),
        "z-": (dp, ((z + 7) % 8) * 2 + yl),
        "yl": (dp, z * 2 + 1 - yl),
        "x+": (dp_of((x + 1) % 4, yh, core), etp),
        "x-": (dp_of((x + 3) % 4, yh, core), etp),
        "y2": (dp_of(x, 1 - yh, core), etp),
        "c": (dp_of(x, yh, 1 - core), etp),
    }
    barrier = pltpu.get_barrier_semaphore()
    for name in dev:
        pl.semaphore_signal(barrier, inc=1, device_id=dev[name], device_id_type=MESH)

    loads = []

    def load(src, dst):
        cp = pltpu.make_async_copy(src, dst, w_sem.at[len(loads)])
        cp.start()
        loads.append(cp)

    load(tokens_h, tokens)
    load(out_grad_h, out_grad)

    count = [0]
    sent, free = [], list(range(s_sem.shape[0]))

    def drain():
        for cp, k in sent:
            cp.wait_send()
            free.append(k)
        sent.clear()

    def send(name, src, dst):
        i, k = count[0], free.pop(0)
        count[0] += 1
        cp = pltpu.make_async_remote_copy(
            src_ref=src, dst_ref=dst, send_sem=s_sem.at[k], recv_sem=r_sem.at[i],
            device_id=dev[name], device_id_type=MESH,
        )
        cp.start()
        sent.append((cp, k))
        return cp

    with jax.named_scope("pack"):
        sel = routed_rows(ids)
        sel_b = sel.astype(BF)
        w_own = jnp.sum(sel * prob[...].astype(F32), axis=1, keepdims=True)
        ds[0:CAP, D:] = jnp.broadcast_to(w_own, (CAP, 128)).astype(BF)
        loads[0].wait()
        xs[0:CAP, :] = dot(sel_b, tokens[...]).astype(BF)
        loads[1].wait()
        ds[0:CAP, 0:D] = dot(sel_b, out_grad[...]).astype(BF)
        load(w_gate_h, wg)
        load(w_up_h, wu)
        load(w_down_h, wd)

    with jax.named_scope("barrier_wait"):
        pl.semaphore_wait(barrier, len(dev))

    arriving = {}

    def gsend(name, key, to, parts="xd"):
        a, b = pl.ds(SLOT[key] * CAP, CAP), pl.ds(SLOT[to] * CAP, CAP)
        for part in parts:
            buf = xs if part == "x" else ds
            arriving[to + (part,)] = send(name, buf.at[a, :], buf.at[b, :])

    def gwait(*keys, parts="xd"):
        for key in keys:
            for part in parts:
                arriving[key + (part,)].wait_recv()

    def forward(g):
        rows = slice(g * 128, (g + 1) * 128)
        wcol = ds[rows, D:].astype(F32)[:, 0:1]
        n_f = 2
        fw_ = F // n_f
        psum = jnp.zeros((128, 1), F32)
        for f in range(n_f):
            cols = slice(f * fw_, (f + 1) * fw_)
            gate = dot(xs[rows, :], wg[:, cols])
            up = dot(xs[rows, :], wu[:, cols])
            raw = dot_t(ds[rows, 0:D], wd[cols, :])
            sig = 1.0 / (1.0 + jnp.exp(-gate))
            act = gate * sig
            hid = (act * up).astype(BF).astype(F32)
            gh = wcol * raw
            gs[2, rows, cols] = (wcol * hid).astype(BF)
            gs[0, rows, cols] = (gh * up * sig * (1.0 + gate * (1.0 - sig))).astype(BF)
            gs[1, rows, cols] = (gh * act).astype(BF)
            psum = psum + jnp.sum(hid * raw, axis=1, keepdims=True)
        pbr = jnp.broadcast_to(psum, (128, 128))
        for q in range(4):
            r = pair_row(*ORDER[4 * g + q])
            pb[r : r + CAP, :] = pbr[q * CAP : (q + 1) * CAP, :]

    def token_part(g):
        rows = slice(g * 128, (g + 1) * 128)

        def tok_tile(n, carry):
            at = pl.multiple_of(n * 512, 512)
            t = (
                dot(gs[0, rows, :], wgt[:, pl.ds(at, 512)])
                + dot(gs[1, rows, :], wut[:, pl.ds(at, 512)])
            ).astype(BF)
            for q in range(4):
                r = pair_row(*ORDER[4 * g + q])
                tp[r : r + CAP, pl.ds(at, 512)] = t[q * CAP : (q + 1) * CAP, :]
            return carry

        lax.fori_loop(0, D // 512, tok_tile, 0)

    def turn(g, src, dst):
        rows = slice(g * 128, (g + 1) * 128)

        def body(n, carry):
            at = pl.multiple_of(n * 256, 256)
            dst[pl.ds(at, 256), rows] = src[rows, pl.ds(at, 256)].T
            return carry

        lax.fori_loop(0, D // 256, body, 0)

    def compute(g):
        with jax.named_scope("forward_g%d" % g):
            forward(g)
        with jax.named_scope("token_g%d" % g):
            token_part(g)
        with jax.named_scope("turn_g%d" % g):
            turn(g, xs, xt)
            turn(g, ds, dt)

    def add_rows(dst, dst_row, src, n, cols):
        def body(i, carry):
            a = pl.ds(pl.multiple_of(dst_row + i * 16, 16), 16)
            b = pl.ds(pl.multiple_of(i * 16, 16), 16)
            dst[a, cols] = (dst[a, cols].astype(F32) + src[b, :].astype(F32)).astype(BF)
            return carry

        lax.fori_loop(0, n // 16, body, 0)

    chain = {}

    def tok_step(c, k):
        for i, name, sign in ((0, "z+", -1), (1, "z-", 1)):
            r = pair_row(c, sign * k)
            mine = pl.ds(r, CAP)
            pair = pair_row(0, sign * k)
            both = slice(pair, pair + 2 * CAP)
            gotp = None
            if k == 4:
                cols = slice(0, H) if i == 0 else slice(H, D)
                got = send(name, tp.at[mine, cols], rph.at[i, c])
                if c == 1 and i == 0:
                    gotp = send(name, pb.at[both, :], pr.at[i, 0])
            else:
                before_t, before_p = chain[name, c, k + 1]
                before_t.wait_recv()
                if k == 3:
                    cols = slice(0, H) if i == 0 else slice(H, D)
                    add_rows(tp, r, rph.at[i, c], CAP, cols)
                else:
                    add_rows(tp, r, rp.at[i, c, 2 - k], CAP, slice(0, D))
                got = send(name, tp.at[mine, :], rp.at[i, c, 3 - k])
                if c == 1:
                    if before_p is not None:
                        before_p.wait_recv()
                        pb[both, :] = pb[both, :] + pr[i, 3 - k]
                    gotp = send(name, pb.at[both, :], pr.at[i, 4 - k])
            chain[name, c, k] = (got, gotp)

    def tok_arrived(c):
        for name in ("z+", "z-"):
            for cp in chain[name, c, 1]:
                if cp is not None:
                    cp.wait_recv()

    own_rows, other_rows = slice(0, CAP), slice(CAP, 2 * CAP)

    def tok_cross():
        tok_arrived(1)

        def body(i, carry):
            a = pl.ds(pl.multiple_of(CAP + i * 16, 16), 16)
            b = pl.ds(pl.multiple_of(i * 16, 16), 16)
            tp[a, :] = (
                tp[a, :].astype(F32) + rp[0, 1, 2, b, :].astype(F32) + rp[1, 1, 2, b, :].astype(F32)
            ).astype(BF)
            return carry

        lax.fori_loop(0, CAP // 16, body, 0)
        t = send("yl", tp.at[pl.ds(CAP, CAP), :], ry)
        pb[other_rows, :] = pb[other_rows, :] + pr[0, 3, other_rows] + pr[1, 3, other_rows]
        p = send("yl", pb.at[pl.ds(CAP, CAP), :], pry)
        return t, p

    def tok_final(t, p):
        tok_arrived(0)
        t.wait_recv()
        p.wait_recv()

        def body(i, carry):
            a = pl.ds(pl.multiple_of(i * 16, 16), 16)
            ry[a, :] = (
                tp[a, :].astype(F32) + rp[0, 0, 2, a, :].astype(F32)
                + rp[1, 0, 2, a, :].astype(F32) + ry[a, :].astype(F32)
            ).astype(BF)
            return carry

        lax.fori_loop(0, CAP // 16, body, 0)
        pry[...] = pb[own_rows, :] + pr[0, 3, own_rows] + pr[1, 3, own_rows] + pry[...]
        out(0, ry, o_tok)
        out(1, pry, o_prob)

    outs = []

    def out(i, src, dst):
        cp = pltpu.make_async_copy(src, dst, o_sem.at[i])
        cp.start()
        outs.append(cp)

    def chunk_dot(key, pc, p):
        dx, h = key
        owner = dp_of((x + dx + 4) % 4, (yh + h) % 2, pc)
        at = pl.multiple_of(owner * rows_own, 64)
        lhs = dt if p == 2 else xt
        return dot(lhs[pl.ds(at, rows_own), :], gs[p])

    from_core = {}
    met = set()

    def sib(p, *keys):
        for key in keys:
            ws[p, CIDX[key]] = chunk_dot(key, 1 - core, p).astype(BF)
        at = pl.ds(CIDX[keys[0]], len(keys))
        cp = send("c", ws.at[p, at], sr.at[p, at])
        for key in keys:
            from_core[key, p] = cp

    def own(p, *keys):
        for key in keys:
            i = CIDX[key]
            v = chunk_dot(key, core, p)
            cp = from_core[key, p]
            if id(cp) not in met:
                met.add(id(cp))
                cp.wait_recv()
            sr[p, i] = (v + sr[p, i].astype(F32)).astype(BF)

    far = {}

    def far_send(h, p):
        i = CIDX[(2, h)]
        for s, name in ((0, "x+"), (1, "x-")):
            far[name, h, p] = send(name, sr.at[p, i, pl.ds(s * half, half), :], xa.at[s, h, p])

    near = {}

    def near_send(h, p):
        for s, name, dx in ((0, "x+", 1), (1, "x-", -1)):
            far[name, h, p].wait_recv()
            i = CIDX[(dx, h)]
            r = slice(s * half, (s + 1) * half)
            sr[p, i, r, :] = (sr[p, i, r, :].astype(F32) + xa[s, h, p].astype(F32)).astype(BF)
            near[name, h, p] = send(name, sr.at[p, i], xb.at[s, h, p])

    def near_wait(h, p):
        for name in ("x+", "x-"):
            near[name, h, p].wait_recv()

    to_y = {}

    def y_last(p):
        near_wait(1, p)
        i = CIDX[(0, 1)]
        sr[p, i] = (
            sr[p, i].astype(F32) + xb[0, 1, p].astype(F32) + xb[1, 1, p].astype(F32)
        ).astype(BF)
        to_y[p] = send("y2", sr.at[p, i], yb.at[p])

    def y_first(dx):
        to_y[2, dx] = send("y2", sr.at[2, CIDX[(dx, 1)]], yc.at[CIDX[(dx, 0)] // 2])

    def y_add(dx):
        to_y[2, dx].wait_recv()
        i = CIDX[(dx, 0)]
        sr[2, i] = (sr[2, i].astype(F32) + yc[i // 2].astype(F32)).astype(BF)

    def w_final(p):
        near_wait(0, p)
        i = CIDX[(0, 0)]
        total = sr[p, i].astype(F32) + xb[0, 0, p].astype(F32) + xb[1, 0, p].astype(F32)
        if p < 2:
            to_y[p].wait_recv()
            total = total + yb[p].astype(F32)
        fw[p] = (total * (1.0 / 16.0)).astype(BF)
        out(2 + p, fw.at[p], o_w.at[p])

    scope = jax.named_scope

    gsend("z+", (0, 0), (0, 1))
    gsend("z-", (0, 0), (0, -1))
    gsend("yl", (0, 0), (1, 0))
    with scope("wait_weights"):
        for cp in loads[2:]:
            cp.wait()
    with scope("turn_weights"):
        def turn_weights(n, carry):
            at = pl.multiple_of(n * 256, 256)
            wgt[:, pl.ds(at, 256)] = wg[pl.ds(at, 256), :].T
            wut[:, pl.ds(at, 256)] = wu[pl.ds(at, 256), :].T
            return carry

        lax.fori_loop(0, D // 256, turn_weights, 0)
    with scope("wait_1"):
        for part in "xd":
            gwait((0, 1), parts=part)
            gsend("z+", (0, 1), (0, 2), part)
            gsend("yl", (0, 1), (1, 1), part)
            gwait((0, -1), parts=part)
            gsend("z-", (0, -1), (0, -2), part)
            gsend("yl", (0, -1), (1, -1), part)
        gwait((1, 0))
    compute(0)
    with scope("wait_2"):
        for part in "xd":
            gwait((0, 2), parts=part)
            gsend("z+", (0, 2), (0, 3), part)
            gwait((0, -2), parts=part)
            gsend("z-", (0, -2), (0, -3), part)
    with scope("wait_y_x"):
        gwait((1, 1), (1, -1), parts="x")
        gsend("yl", (0, 2), (1, 2), "x")
        gsend("yl", (0, -2), (1, -2), "x")
    with scope("wait_3"):
        gwait((0, 3), parts="x")
        gsend("z+", (0, 3), (0, 4), "x")
        gwait((0, -3), parts="d")
        gsend("z-", (0, -3), (0, 4), "d")
        gwait((1, 1), parts="d")
        gsend("z+", (1, 1), (1, 2), "d")
        gwait((1, -1), parts="d")
        gsend("z-", (1, -1), (1, -2), "d")
    compute(1)
    with scope("wait_4"):
        gwait((0, 4))
        gsend("yl", (0, 4), (1, 4))
    with scope("wait_5"):
        for part in "xd":
            gwait((1, 2), parts=part)
            gsend("z+", (1, 2), (1, 3), part)
            gwait((1, -2), parts=part)
            gsend("z-", (1, -2), (1, -3), part)
        gwait((0, 3), parts="d")
        gwait((0, -3), parts="x")
    compute(2)
    with scope("wait_6x"):
        gwait((1, 3), (1, -3), (1, 4), parts="x")
    with scope("turn_x"):
        turn(3, xs, xt)
    with scope("wait_6d"):
        gwait((1, 3), (1, -3), (1, 4), parts="d")
    with scope("forward_g3"):
        forward(3)
    with scope("drain_gather"):
        drain()
    tok_step(0, 4)
    with scope("chunks_a"):
        sib(0, (2, 0), (2, 1))
        turn(3, ds, dt)
        sib(2, (2, 1))
        sib(2, (1, 1))
        own(0, (2, 1))
        far_send(1, 0)
        own(0, (2, 0))
        far_send(0, 0)
        own(2, (2, 1))
        y_first(2)
        own(2, (1, 1))
        y_first(1)
    with scope("tok_0_3"):
        tok_step(0, 3)
    with scope("token_g3"):
        token_part(3)
    tok_step(1, 4)
    with scope("chunks_b"):
        sib(1, (2, 0), (2, 1))
        sib(0, (1, 0), (1, 1), (-1, 0), (-1, 1))
        sib(2, (-1, 1))
        sib(2, (0, 1))
        own(1, (2, 1))
        far_send(1, 1)
        own(1, (2, 0))
        far_send(0, 1)
        own(0, (1, 1), (-1, 1))
    with scope("near_h1_p0"):
        near_send(1, 0)
    with scope("tok_0_2"):
        own(0, (1, 0), (-1, 0))
        tok_step(0, 2)
    with scope("near_h0_p0"):
        near_send(0, 0)
    with scope("y_first_rest"):
        own(2, (-1, 1))
        y_first(-1)
        own(2, (0, 1))
        y_first(0)
    with scope("tok_1_3"):
        tok_step(1, 3)
    with scope("chunks_c"):
        sib(1, (1, 0), (1, 1), (-1, 0), (-1, 1))
        sib(2, (2, 0))
        sib(2, (1, 0))
        sib(2, (-1, 0))
        sib(0, (0, 0), (0, 1))
        sib(1, (0, 0), (0, 1))
        sib(2, (0, 0))
        own(2, (2, 0))
    with scope("y_add_2"):
        y_add(2)
        far_send(0, 2)
    with scope("chunks_d"):
        own(1, (1, 1), (-1, 1), (1, 0), (-1, 0))
    with scope("near_h1_p1"):
        near_send(1, 1)
    with scope("near_h0_p1"):
        near_send(0, 1)
    with scope("chunks_e"):
        own(2, (1, 0), (-1, 0), (0, 0))
        own(0, (0, 1), (0, 0))
        own(1, (0, 1), (0, 0))
    with scope("tok_0_1"):
        tok_step(0, 1)
    with scope("tok_1_2"):
        tok_step(1, 2)
    with scope("y_add_near"):
        y_add(1)
        y_add(-1)
    with scope("near_h0_p2"):
        near_send(0, 2)
    with scope("y_last_0"):
        y_last(0)
    with scope("y_add_0"):
        y_add(0)
    with scope("tok_1_1"):
        tok_step(1, 1)
    with scope("y_last_1"):
        y_last(1)
    with scope("tok_cross"):
        t, q = tok_cross()
    with scope("w_final_0"):
        w_final(0)
    with scope("w_final_1"):
        w_final(1)
    with scope("w_final_2"):
        w_final(2)
    with scope("tok_final"):
        tok_final(t, q)
    with scope("drain"):
        drain()
        for cp in outs:
            cp.wait()


def finish(ids, packed, psum, w_in, o_tok, o_prob, o_gate, o_up, o_down):
    sel = routed_rows(ids)
    o_gate[...] = w_in[0]
    o_up[...] = w_in[1]
    o_down[...] = w_in[2]
    o_tok[...] = dot(sel.T.astype(BF), packed[...]).astype(BF)
    o_prob[...] = jnp.sum(sel * psum[...], axis=0, keepdims=True)


def shards(tokens, out_grad, route_ids, route_prob, w_gate, w_up, w_down):
    n_tok, D = tokens.shape
    F = w_gate.shape[1]
    own = D // lax.axis_size("dp")
    rows = CAP * lax.axis_size("etp")
    vmem = pl.BlockSpec(memory_space=pltpu.VMEM)
    hbm = pl.BlockSpec(memory_space=pl.ANY)
    n_send, n_recv = 65, 95
    scratch = [
        pltpu.VMEM((n_tok, D), BF),
        pltpu.VMEM((n_tok, D), BF),
        pltpu.VMEM((D, F), BF),
        pltpu.VMEM((D, F), BF),
        pltpu.VMEM((F, D), BF),
        pltpu.VMEM((F, D), BF),
        pltpu.VMEM((F, D), BF),
        pltpu.VMEM((rows, D), BF),
        pltpu.VMEM((rows, D + 128), BF),
        pltpu.VMEM((D, rows), BF),
        pltpu.VMEM((D, rows), BF),
        pltpu.VMEM((3, rows, F), BF),
        pltpu.VMEM((rows, D), BF),
        pltpu.VMEM((rows, 128), F32),
        pltpu.VMEM((3, 8, own, F), BF),
        pltpu.VMEM((3, 8, own, F), BF),
        pltpu.VMEM((2, 2, 3, own // 2, F), BF),
        pltpu.VMEM((2, 2, 3, own, F), BF),
        pltpu.VMEM((2, own, F), BF),
        pltpu.VMEM((4, own, F), BF),
        pltpu.VMEM((2, 2, 3, CAP, D), BF),
        pltpu.VMEM((2, 2, CAP, D // 2), BF),
        pltpu.VMEM((2, 4, 2 * CAP, 128), F32),
        pltpu.VMEM((CAP, D), BF),
        pltpu.VMEM((CAP, 128), F32),
        pltpu.VMEM((3, own, F), BF),
        pltpu.SemaphoreType.DMA((5,)),
        pltpu.SemaphoreType.DMA((5,)),
        pltpu.SemaphoreType.DMA((n_send,)),
        pltpu.SemaphoreType.DMA((n_recv,)),
    ]
    ids = route_ids.T
    packed, psum, g_w = pl.pallas_call(
        kernel,
        out_shape=(
            jax.ShapeDtypeStruct((CAP, D), BF),
            jax.ShapeDtypeStruct((CAP, 128), F32),
            jax.ShapeDtypeStruct((3, own, F), BF),
        ),
        in_specs=[vmem] * 2 + [hbm] * 5,
        out_specs=(hbm, hbm, hbm),
        scratch_shapes=scratch,
        compiler_params=pltpu.CompilerParams(
            collective_id=0, has_side_effects=True, vmem_limit_bytes=60 * 1024 * 1024
        ),
        cost_estimate=pl.CostEstimate(
            flops=8 * 2 * rows * D * F, bytes_accessed=6 * D * F + 8 * n_tok * D, transcendentals=rows * F
        ),
    )(ids, route_prob.reshape(1, n_tok), tokens, out_grad, w_gate, w_up, w_down)
    g_tok, g_prob, g_gate, g_up, g_down = pl.pallas_call(
        finish,
        out_shape=(
            jax.ShapeDtypeStruct((n_tok, D), BF),
            jax.ShapeDtypeStruct((1, n_tok), F32),
        )
        + (jax.ShapeDtypeStruct((own, F), BF),) * 3,
        in_specs=[vmem] * 4,
        out_specs=(vmem,) * 5,
    )(ids, packed, psum, g_w)
    return g_tok, g_prob.reshape(n_tok), g_gate, g_up, g_down.T


def solution(mesh):
    placed = (
        P(("dp", "etp"), None),
        P(("dp", "etp"), None),
        P(("dp", "etp"), None),
        P(("dp", "etp")),
        P(None, "etp"),
        P(None, "etp"),
        P("etp", None),
    )
    return jax.shard_map(
        shards,
        mesh=mesh,
        in_specs=placed,
        out_specs=(
            P(("dp", "etp"), None),
            P(("dp", "etp")),
            P("dp", "etp"),
            P("dp", "etp"),
            P("etp", "dp"),
        ),
        check_vma=False,
    )
```

time: 116 us -> 106 us (0.914); the launches traced: 114 us -> 106 us
  local copies, waits for them, and re-layouts: 5.08 us -> 0 us
  Pallas kernels: 108 us -> 105 us
    unnamed x2 -> x0, local copies, waits for them, and re-layouts: 3.14 us -> none
    pallas_call x1 -> x2, Pallas kernels: 108 us -> 105 us  [the longest x1 102 us: shards(): pl.pallas_call(kernel, out_shape=(jax.ShapeDtypeStruct((CAP, D), BF), jax...]
    transpose x1 -> x0, local copies, waits for them, and re-layouts: 1.94 us -> none  [shards(): return (g_tok, g_prob.reshape(n_tok), g_w[0], g_w[1], g_w[2].T)]
where the time goes in v2:
time: 106 us
  Pallas kernels  105 us (99%)
    pallas_call x1, Pallas kernels, shards(): pl.pallas_call(kernel, out_shape=(jax.ShapeDtypeStruct((CAP, D), BF), jax...  102 us
    pallas_call x1, Pallas kernels, shards(): pl.pallas_call(finish, out_shape=(jax.ShapeDtypeStruct((n_tok, D), BF), j...  2.77 us

profile of v2, /device:TPU:1, one launch (start us, length us, event | category | flops | bytes accessed | tf_op | source)
XLA Modules:
  0.0 105.9 jit_solution(2298883991488473987)
XLA Ops:
  0.6 102.5 %shard_map.110 = (bf16[32,3072]{1,0:T(8,128)(2,1)}, f32[32,128]{1,0:T(8,128)}, bf16[3,192,512]{2,1,0:T(8,128)(2,1)}) custom-call(s32[2,128]{1,0:T(2,128)} %bitcast.4, bf16[1,128]{1,0:T(2,128)(2,1)} %bitcast.7, bf16[128,3072]{1,0:T(8,128)(2,1)} %tokens_h.1, bf16[128,3072]{1,0:T(8,128)(2,1)} %out_grad_h.1, bf16[3072,512]{1,0:T(8,128)(2,1)} %w_gate_h.1, ...), custom_call_target="tpu_custom_call" | custom-call | flops 12884901888 | bytes 12582912 | tf_op jit(solution)/shard_map/pallas_call | solution.py:590
  103.1 2.8 %shard_map.111 = (bf16[128,3072]{1,0:T(8,128)(2,1)}, f32[1,128]{1,0:T(1,128)}, bf16[192,512]{1,0:T(8,128)(2,1)}, bf16[192,512]{1,0:T(8,128)(2,1)}, bf16[192,512]{1,0:T(8,128)(2,1)}) custom-call(s32[2,128]{1,0:T(2,128)} %bitcast.5, bf16[32,3072]{1,0:T(8,128)(2,1)} %get-tuple-element.13.packed, f32[32,128]{1,0:T(8,128)} %get-tuple-element.14.psum, ...), custom_call_target="tpu_custom_call" | custom-call | tf_op jit(solution)/shard_map/pallas_call | solution.py:607

commit v3 on v2

v3 whole, which is shorter than its diff:
```python
import functools

import jax
import jax.numpy as jnp
from jax import lax
from jax.experimental import pallas as pl
from jax.experimental.pallas import tpu as pltpu
from jax.sharding import PartitionSpec as P

MESH = pl.DeviceIdType.MESH
CAP = 32
BF = jnp.bfloat16
F32 = jnp.float32

ORDER = (
    (0, 0), (1, 0), (0, 1), (0, -1),
    (0, 2), (0, -2), (1, 1), (1, -1),
    (0, 3), (0, -3), (1, 2), (1, -2),
    (0, 4), (1, 3), (1, -3), (1, 4),
)
HALF = CAP // 2
SLOT = {key: i for i, key in enumerate(ORDER)}
CHUNKS = ((2, 0), (2, 1), (1, 0), (1, 1), (-1, 0), (-1, 1), (0, 0), (0, 1))
CIDX = {key: i for i, key in enumerate(CHUNKS)}


def pair_row(col, off):
    return ((off % 8) * 2 + col) * CAP


def dot(a, b):
    return jnp.dot(a, b, preferred_element_type=F32)


def dot_t(a, b):
    return lax.dot_general(a, b, (((1,), (1,)), ((), ())), preferred_element_type=F32)


def routed_rows(ids):
    routed = jnp.logical_or(ids[0:1, :] == 0, ids[1:2, :] == 0)
    n_tok = routed.shape[1]
    routed_f = jnp.where(routed, 1.0, 0.0).astype(F32)
    before = (
        lax.broadcasted_iota(jnp.int32, (n_tok, n_tok), 0)
        < lax.broadcasted_iota(jnp.int32, (n_tok, n_tok), 1)
    )
    rank = dot(
        jnp.broadcast_to(routed_f, (16, n_tok)).astype(BF),
        jnp.where(before, 1.0, 0.0).astype(BF),
    )[0:1, :]
    slot_no = lax.broadcasted_iota(jnp.int32, (CAP, n_tok), 0).astype(F32)
    chosen = jnp.logical_and(
        jnp.broadcast_to(rank, (CAP, n_tok)) == slot_no,
        jnp.broadcast_to(routed_f, (CAP, n_tok)) > 0.5,
    )
    return jnp.where(chosen, 1.0, 0.0).astype(F32)


def kernel(
    ids_h, prob_h, tokens_h, out_grad_h, w_gate_h, w_up_h, w_down_h,
    o_tok, o_prob, o_w,
    ids, prob, tokens, out_grad, wg, wu, wd, wgt, wut, xs, ds, xt, dt, gs, tp, pb, ws, sr, xa, xb, yb, yc,
    rp, rph, pr, ry, pry, fw,
    w_sem, o_sem, s_sem, r_sem,
):
    D = xs.shape[1]
    F = wg.shape[1]
    H = D // 2
    rows_own = fw.shape[1]
    half = rows_own // 2
    dp, etp = lax.axis_index("dp"), lax.axis_index("etp")
    x, yh, core = dp // 4, (dp // 2) % 2, dp % 2
    z, yl = etp // 2, etp % 2

    def dp_of(px, ph, pc):
        return px * 4 + ph * 2 + pc

    def y_at(step):
        y = (yh * 2 + yl + step) % 4
        return dp_of(x, y // 2, core), z * 2 + y % 2

    dev = {
        "z+": (dp, ((z + 1) % 8) * 2 + yl),
        "z-": (dp, ((z + 7) % 8) * 2 + yl),
        "y+": y_at(1),
        "y-": y_at(3),
        "x+": (dp_of((x + 1) % 4, yh, core), etp),
        "x-": (dp_of((x + 3) % 4, yh, core), etp),
        "y2": (dp_of(x, 1 - yh, core), etp),
        "c": (dp_of(x, yh, 1 - core), etp),
    }
    barrier = pltpu.get_barrier_semaphore()
    for name in dev:
        pl.semaphore_signal(barrier, inc=1, device_id=dev[name], device_id_type=MESH)

    loads = []

    def load(src, dst):
        cp = pltpu.make_async_copy(src, dst, w_sem.at[len(loads)])
        cp.start()
        loads.append(cp)

    load(ids_h, ids)
    load(prob_h, prob)
    load(tokens_h, tokens)
    load(out_grad_h, out_grad)

    count = [0]
    sent, free = [], list(range(s_sem.shape[0]))

    def drain(n):
        for cp, k in sent[:n]:
            cp.wait_send()
            free.append(k)
        del sent[:n]

    def send(name, src, dst):
        return send_all([(name, src, dst)], src, dst)

    def send_all(items, src, dst):
        i, k = count[0], free.pop(0)
        count[0] += 1

        def copy(name, a, b):
            return pltpu.make_async_remote_copy(
                src_ref=a, dst_ref=b, send_sem=s_sem.at[k], recv_sem=r_sem.at[i],
                device_id=dev[name], device_id_type=MESH,
            )

        for item in items:
            copy(*item).start()
        whole = copy(items[0][0], src, dst)
        sent.append((whole, k))
        return whole

    with jax.named_scope("pack"):
        loads[0].wait()
        sel = routed_rows(ids)
        sel_b = sel.astype(BF)
        loads[1].wait()
        w_own = jnp.sum(sel * prob[...].astype(F32), axis=1, keepdims=True)
        ds[0:CAP, D:] = jnp.broadcast_to(w_own, (CAP, 128)).astype(BF)
        loads[2].wait()
        xs[0:CAP, :] = dot(sel_b, tokens[...]).astype(BF)
        loads[3].wait()
        ds[0:CAP, 0:D] = dot(sel_b, out_grad[...]).astype(BF)
        load(w_gate_h, wg)
        load(w_up_h, wu)
        load(w_down_h, wd)

    with jax.named_scope("barrier_wait"):
        pl.semaphore_wait(barrier, len(dev))

    arriving = {}

    def gsend(name, key, to, part):
        a, b = pl.ds(SLOT[key] * CAP, CAP), pl.ds(SLOT[to] * CAP, CAP)
        buf = xs if part == "x" else ds
        arriving[to + (part,)] = send(name, buf.at[a, :], buf.at[b, :])

    def ysend(off, part):
        buf = xs if part == "x" else ds
        a, b = SLOT[(0, off)] * CAP, SLOT[(1, off)] * CAP
        arriving[(1, off, part)] = send_all(
            [
                (name, buf.at[pl.ds(a + q * HALF, HALF), :], buf.at[pl.ds(b + q * HALF, HALF), :])
                for q, name in ((0, "y+"), (1, "y-"))
            ],
            buf.at[pl.ds(a, CAP), :],
            buf.at[pl.ds(b, CAP), :],
        )

    def gwait(*keys, parts="xd"):
        for key in keys:
            for part in parts:
                arriving.pop(key + (part,)).wait_recv()

    def relay(dist, part):
        for name, sign in (("z+", 1), ("z-", -1)):
            key = (0, sign * dist)
            gwait(key, parts=part)
            if dist < 3:
                gsend(name, key, (0, sign * (dist + 1)), part)
            elif (name, part) in (("z+", "x"), ("z-", "d")):
                gsend(name, key, (0, 4), part)
            ysend(sign * dist, part)

    def forward(first, n):
        m = n * CAP
        rows = slice(first * CAP, first * CAP + m)
        wcol = ds[rows, D:].astype(F32)[:, 0:1]
        n_f = 2
        fw_ = F // n_f
        psum = jnp.zeros((m, 1), F32)
        for f in range(n_f):
            cols = slice(f * fw_, (f + 1) * fw_)
            gate = dot(xs[rows, :], wg[:, cols])
            up = dot(xs[rows, :], wu[:, cols])
            raw = dot_t(ds[rows, 0:D], wd[cols, :])
            sig = 1.0 / (1.0 + jnp.exp(-gate))
            act = gate * sig
            hid = (act * up).astype(BF).astype(F32)
            gh = wcol * raw
            gs[2, rows, cols] = (wcol * hid).astype(BF)
            gs[0, rows, cols] = (gh * up * sig * (1.0 + gate * (1.0 - sig))).astype(BF)
            gs[1, rows, cols] = (gh * act).astype(BF)
            psum = psum + jnp.sum(hid * raw, axis=1, keepdims=True)
        pbr = jnp.broadcast_to(psum, (m, 128))
        for q in range(n):
            r = pair_row(*ORDER[first + q])
            pb[r : r + CAP, :] = pbr[q * CAP : (q + 1) * CAP, :]

    def token_part(first, n, skip=()):
        rows = slice(first * CAP, (first + n) * CAP)

        def tok_tile(i, carry):
            at = pl.multiple_of(i * 512, 512)
            t = (
                dot(gs[0, rows, :], wgt[:, pl.ds(at, 512)])
                + dot(gs[1, rows, :], wut[:, pl.ds(at, 512)])
            ).astype(BF)
            for q in range(n):
                if ORDER[first + q] in skip:
                    continue
                r = pair_row(*ORDER[first + q])
                tp[r : r + CAP, pl.ds(at, 512)] = t[q * CAP : (q + 1) * CAP, :]
            return carry

        lax.fori_loop(0, D // 512, tok_tile, 0)

    def turn(g, src, dst):
        rows = slice(g * 128, (g + 1) * 128)

        def body(n, carry):
            at = pl.multiple_of(n * 256, 256)
            dst[pl.ds(at, 256), rows] = src[rows, pl.ds(at, 256)].T
            return carry

        lax.fori_loop(0, D // 256, body, 0)

    def add_rows(dst, dst_row, src, n, cols):
        def body(i, carry):
            a = pl.ds(pl.multiple_of(dst_row + i * 16, 16), 16)
            b = pl.ds(pl.multiple_of(i * 16, 16), 16)
            dst[a, cols] = (dst[a, cols].astype(F32) + src[b, :].astype(F32)).astype(BF)
            return carry

        lax.fori_loop(0, n // 16, body, 0)

    chain = {}

    def tok_step(c, k):
        sides = ((0, "z+", -1), (1, "z-", 1))
        rows = [pair_row(c, sign * k) for _, _, sign in sides]
        pairs = [pair_row(0, sign * k) for _, _, sign in sides]
        pair = 2 * CAP
        if k < 4:
            before_t, before_p = chain[c, k + 1]
            before_t.wait_recv()
        if k == 4:
            got = send_all(
                [
                    (name, tp.at[pl.ds(rows[i], CAP), slice(i * H, (i + 1) * H)], rph.at[i, c])
                    for i, name, _ in sides
                ],
                tp.at[pl.ds(rows[0], CAP), :],
                tp.at[pl.ds(rows[0], CAP), :],
            )
        else:
            for i, _, _ in sides:
                if k == 3:
                    add_rows(tp, rows[i], rph.at[i, c], CAP, slice(i * H, (i + 1) * H))
                else:
                    add_rows(tp, rows[i], rp.at[c, 2 - k, i], CAP, slice(0, D))
            got = send_all(
                [(name, tp.at[pl.ds(rows[i], CAP), :], rp.at[c, 3 - k, i]) for i, name, _ in sides],
                rp.at[c, 3 - k],
                rp.at[c, 3 - k],
            )
        gotp = None
        if c == 1:
            if k == 4:
                gotp = send("z+", pb.at[pl.ds(pairs[0], pair), :], pr.at[0, 0])
            else:
                before_p.wait_recv()
                for i in (0, 1) if k < 3 else (0,):
                    both = slice(pairs[i], pairs[i] + pair)
                    pb[both, :] = pb[both, :] + pr[3 - k, i]
                gotp = send_all(
                    [
                        (name, pb.at[pl.ds(pairs[i], pair), :], pr.at[4 - k, i])
                        for i, name, _ in sides
                    ],
                    pr.at[4 - k],
                    pr.at[4 - k],
                )
        chain[c, k] = (got, gotp)

    def tok_arrived(c):
        for cp in chain[c, 1]:
            if cp is not None:
                cp.wait_recv()

    own_rows, other_rows = slice(0, CAP), slice(CAP, 2 * CAP)

    def tok_cross():
        tok_arrived(1)

        def body(i, carry):
            a = pl.ds(pl.multiple_of(CAP + i * 16, 16), 16)
            b = pl.ds(pl.multiple_of(i * 16, 16), 16)
            tp[a, :] = (
                tp[a, :].astype(F32) + rp[1, 2, 0, b, :].astype(F32) + rp[1, 2, 1, b, :].astype(F32)
            ).astype(BF)
            return carry

        lax.fori_loop(0, CAP // 16, body, 0)
        pb[other_rows, :] = pb[other_rows, :] + pr[3, 0, other_rows] + pr[3, 1, other_rows]
        crossing = []
        for src, dst in ((tp, ry), (pb, pry)):
            crossing.append(
                send_all(
                    [
                        (name, src.at[pl.ds(CAP + q * HALF, HALF), :], dst.at[pl.ds(q * HALF, HALF), :])
                        for q, name in ((0, "y-"), (1, "y+"))
                    ],
                    src.at[pl.ds(CAP, CAP), :],
                    dst,
                )
            )
        return crossing

    def tok_final(crossing):
        tok_arrived(0)
        for cp in crossing:
            cp.wait_recv()

        def body(i, carry):
            a = pl.ds(pl.multiple_of(i * 16, 16), 16)
            ry[a, :] = (
                tp[a, :].astype(F32) + rp[0, 2, 0, a, :].astype(F32)
                + rp[0, 2, 1, a, :].astype(F32) + ry[a, :].astype(F32)
            ).astype(BF)
            return carry

        lax.fori_loop(0, CAP // 16, body, 0)
        pry[...] = pb[own_rows, :] + pr[3, 0, own_rows] + pr[3, 1, own_rows] + pry[...]
        out(0, ry, o_tok)
        out(1, pry, o_prob)

    outs = []

    def out(i, src, dst):
        cp = pltpu.make_async_copy(src, dst, o_sem.at[i])
        cp.start()
        outs.append(cp)

    def chunk_dot(key, pc, p):
        dx, h = key
        owner = dp_of((x + dx + 4) % 4, (yh + h) % 2, pc)
        at = pl.multiple_of(owner * rows_own, 64)
        lhs = dt if p == 2 else xt
        return dot(lhs[pl.ds(at, rows_own), :], gs[p])

    from_core = {}
    met = set()

    def sib(p, *keys):
        for key in keys:
            ws[p, CIDX[key]] = chunk_dot(key, 1 - core, p).astype(BF)
        at = pl.ds(CIDX[keys[0]], len(keys))
        cp = send("c", ws.at[p, at], sr.at[p, at])
        for key in keys:
            from_core[key, p] = cp

    def own(p, *keys):
        for key in keys:
            i = CIDX[key]
            v = chunk_dot(key, core, p)
            cp = from_core[key, p]
            if id(cp) not in met:
                met.add(id(cp))
                cp.wait_recv()
            sr[p, i] = (v + sr[p, i].astype(F32)).astype(BF)

    far = {}

    def far_send(h, p):
        i = CIDX[(2, h)]
        far[h, p] = send_all(
            [
                (name, sr.at[p, i, pl.ds(q * half, half), :], xa.at[h, p, pl.ds(q * half, half), :])
                for q, name in ((0, "x+"), (1, "x-"))
            ],
            sr.at[p, i],
            xa.at[h, p],
        )

    near = {}

    def near_send(h, p):
        far[h, p].wait_recv()
        for q, dx in ((0, 1), (1, -1)):
            i = CIDX[(dx, h)]
            r = slice(q * half, (q + 1) * half)
            sr[p, i, r, :] = (sr[p, i, r, :].astype(F32) + xa[h, p, r, :].astype(F32)).astype(BF)
        near[h, p] = send_all(
            [
                (name, sr.at[p, CIDX[(dx, h)]], xb.at[h, p, q])
                for q, name, dx in ((0, "x+", 1), (1, "x-", -1))
            ],
            xb.at[h, p],
            xb.at[h, p],
        )

    def near_wait(h, p):
        near[h, p].wait_recv()

    to_y = {}

    def y_last(p):
        near_wait(1, p)
        i = CIDX[(0, 1)]
        sr[p, i] = (
            sr[p, i].astype(F32) + xb[1, p, 0].astype(F32) + xb[1, p, 1].astype(F32)
        ).astype(BF)
        to_y[p] = send("y2", sr.at[p, i], yb.at[p])

    def y_first(dx):
        to_y[2, dx] = send("y2", sr.at[2, CIDX[(dx, 1)]], yc.at[CIDX[(dx, 0)] // 2])

    def y_add(dx):
        to_y[2, dx].wait_recv()
        i = CIDX[(dx, 0)]
        sr[2, i] = (sr[2, i].astype(F32) + yc[i // 2].astype(F32)).astype(BF)

    def w_final(p):
        near_wait(0, p)
        i = CIDX[(0, 0)]
        total = sr[p, i].astype(F32) + xb[0, p, 0].astype(F32) + xb[0, p, 1].astype(F32)
        if p < 2:
            to_y[p].wait_recv()
            total = total + yb[p].astype(F32)
        fw[p] = (total * (1.0 / 16.0)).astype(BF)
        out(2 + p, fw.at[p], o_w.at[p])

    scope = jax.named_scope

    for part in "xd":
        gsend("z+", (0, 0), (0, 1), part)
        gsend("z-", (0, 0), (0, -1), part)
        ysend(0, part)
    with scope("wait_weights"):
        for cp in loads[4:]:
            cp.wait()
    with scope("turn_weights"):
        def turn_weights(n, carry):
            at = pl.multiple_of(n * 256, 256)
            wgt[:, pl.ds(at, 256)] = wg[pl.ds(at, 256), :].T
            wut[:, pl.ds(at, 256)] = wu[pl.ds(at, 256), :].T
            return carry

        lax.fori_loop(0, D // 256, turn_weights, 0)
    with scope("relay_1x"):
        relay(1, "x")
    with scope("relay_1d"):
        relay(1, "d")
        gwait((1, 0))
    with scope("forward_g0"):
        forward(0, 4)
    with scope("token_g0"):
        token_part(0, 4)
    with scope("relay_2x"):
        relay(2, "x")
    with scope("turn_g0"):
        turn(0, xs, xt)
        turn(0, ds, dt)
    with scope("relay_2d"):
        relay(2, "d")
    with scope("wait_g1"):
        gwait((1, 1), (1, -1))
    with scope("forward_g1"):
        forward(4, 4)
    with scope("token_g1"):
        token_part(4, 4)
    with scope("relay_3x"):
        relay(3, "x")
    with scope("turn_g1"):
        turn(1, xs, xt)
        turn(1, ds, dt)
    with scope("relay_3d"):
        relay(3, "d")
    with scope("wait_g2"):
        gwait((1, 2), (1, -2))
    with scope("forward_g2"):
        forward(8, 4)
    with scope("turn_g2"):
        turn(2, xs, xt)
        turn(2, ds, dt)
    with scope("relay_4"):
        for part in "xd":
            gwait((0, 4), parts=part)
            ysend(4, part)
    n_gather = len(sent)
    with scope("far_block"):
        forward(12, 1)
        token_part(12, 1)
    tok_step(0, 4)
    with scope("wait_g3x"):
        gwait((1, 3), (1, -3), (1, 4), parts="x")
    with scope("turn_x"):
        turn(3, xs, xt)
    with scope("wait_g3d"):
        gwait((1, 3), (1, -3), (1, 4), parts="d")
    with scope("forward_g3"):
        forward(12, 4)
    with scope("drain_gather"):
        drain(n_gather)
    with scope("chunks_a"):
        sib(0, (2, 0), (2, 1))
    with scope("token_g23"):
        token_part(8, 8, skip=((0, 4),))
    tok_step(1, 4)
    with scope("far_p0"):
        own(0, (2, 1))
        far_send(1, 0)
        own(0, (2, 0))
        far_send(0, 0)
    with scope("turn_d"):
        turn(3, ds, dt)
    with scope("chunks_b"):
        sib(2, (2, 1))
        sib(2, (1, 1))
        sib(1, (2, 0), (2, 1))
        sib(2, (-1, 1))
        sib(2, (0, 1))
    with scope("tok_0_3"):
        tok_step(0, 3)
    with scope("y_first"):
        own(2, (2, 1))
        y_first(2)
        own(2, (1, 1))
        y_first(1)
    with scope("far_p1"):
        own(1, (2, 1))
        far_send(1, 1)
        own(1, (2, 0))
        far_send(0, 1)
    with scope("y_first_b"):
        own(2, (-1, 1))
        y_first(-1)
        own(2, (0, 1))
        y_first(0)
    with scope("tok_1_3"):
        tok_step(1, 3)
    with scope("chunks_c"):
        sib(0, (1, 0), (1, 1), (-1, 0), (-1, 1))
        sib(1, (1, 0), (1, 1), (-1, 0), (-1, 1))
        own(0, (1, 1), (-1, 1), (1, 0), (-1, 0))
    with scope("near_p0"):
        near_send(1, 0)
        near_send(0, 0)
    with scope("chunks_d"):
        sib(2, (2, 0))
        sib(2, (1, 0))
        sib(2, (-1, 0))
    with scope("tok_0_2"):
        tok_step(0, 2)
    with scope("y_add_2"):
        own(2, (2, 0))
        y_add(2)
        far_send(0, 2)
    with scope("chunks_e"):
        own(1, (1, 1), (-1, 1), (1, 0), (-1, 0))
    with scope("near_p1"):
        near_send(1, 1)
        near_send(0, 1)
    with scope("chunks_f"):
        sib(0, (0, 0), (0, 1))
        sib(1, (0, 0), (0, 1))
        sib(2, (0, 0))
        own(2, (1, 0), (-1, 0))
    with scope("tok_1_2"):
        tok_step(1, 2)
    with scope("chunks_g"):
        own(0, (0, 1), (0, 0))
        own(1, (0, 1), (0, 0))
        own(2, (0, 0))
    with scope("y_add_near"):
        y_add(1)
        y_add(-1)
    with scope("y_last_0"):
        y_last(0)
    with scope("tok_1_1"):
        tok_step(1, 1)
    with scope("tok_0_1"):
        tok_step(0, 1)
    with scope("near_p2"):
        near_send(0, 2)
    with scope("y_add_0"):
        y_add(0)
    with scope("tok_cross"):
        crossing = tok_cross()
    with scope("y_last_1"):
        y_last(1)
    with scope("w_final_0"):
        w_final(0)
    with scope("tok_final"):
        tok_final(crossing)
    with scope("w_final_2"):
        w_final(2)
    with scope("w_final_1"):
        w_final(1)
    with scope("drain"):
        drain(len(sent))
        for cp in outs:
            cp.wait()


def finish(ids, packed, psum, w_in, o_tok, o_prob, o_gate, o_up, o_down):
    sel = routed_rows(ids)
    o_gate[...] = w_in[0]
    o_up[...] = w_in[1]
    o_down[...] = w_in[2]
    o_tok[...] = dot(sel.T.astype(BF), packed[...]).astype(BF)
    o_prob[...] = jnp.sum(sel * psum[...], axis=0, keepdims=True)


def shards(tokens, out_grad, route_ids, route_prob, w_gate, w_up, w_down):
    n_tok, D = tokens.shape
    F = w_gate.shape[1]
    own = D // lax.axis_size("dp")
    rows = CAP * lax.axis_size("etp")
    vmem = pl.BlockSpec(memory_space=pltpu.VMEM)
    hbm = pl.BlockSpec(memory_space=pl.ANY)
    n_send, n_recv = 45, 74
    scratch = [
        pltpu.VMEM((2, n_tok), jnp.int32),
        pltpu.VMEM((1, n_tok), BF),
        pltpu.VMEM((n_tok, D), BF),
        pltpu.VMEM((n_tok, D), BF),
        pltpu.VMEM((D, F), BF),
        pltpu.VMEM((D, F), BF),
        pltpu.VMEM((F, D), BF),
        pltpu.VMEM((F, D), BF),
        pltpu.VMEM((F, D), BF),
        pltpu.VMEM((rows, D), BF),
        pltpu.VMEM((rows, D + 128), BF),
        pltpu.VMEM((D, rows), BF),
        pltpu.VMEM((D, rows), BF),
        pltpu.VMEM((3, rows, F), BF),
        pltpu.VMEM((rows, D), BF),
        pltpu.VMEM((rows, 128), F32),
        pltpu.VMEM((3, 8, own, F), BF),
        pltpu.VMEM((3, 8, own, F), BF),
        pltpu.VMEM((2, 3, own, F), BF),
        pltpu.VMEM((2, 3, 2, own, F), BF),
        pltpu.VMEM((2, own, F), BF),
        pltpu.VMEM((4, own, F), BF),
        pltpu.VMEM((2, 3, 2, CAP, D), BF),
        pltpu.VMEM((2, 2, CAP, D // 2), BF),
        pltpu.VMEM((4, 2, 2 * CAP, 128), F32),
        pltpu.VMEM((CAP, D), BF),
        pltpu.VMEM((CAP, 128), F32),
        pltpu.VMEM((3, own, F), BF),
        pltpu.SemaphoreType.DMA((7,)),
        pltpu.SemaphoreType.DMA((5,)),
        pltpu.SemaphoreType.DMA((n_send,)),
        pltpu.SemaphoreType.DMA((n_recv,)),
    ]
    ids = route_ids.T
    packed, psum, g_w = pl.pallas_call(
        kernel,
        out_shape=(
            jax.ShapeDtypeStruct((CAP, D), BF),
            jax.ShapeDtypeStruct((CAP, 128), F32),
            jax.ShapeDtypeStruct((3, own, F), BF),
        ),
        in_specs=[hbm] * 7,
        out_specs=(hbm, hbm, hbm),
        scratch_shapes=scratch,
        compiler_params=pltpu.CompilerParams(
            collective_id=0, has_side_effects=True, vmem_limit_bytes=60 * 1024 * 1024
        ),
        cost_estimate=pl.CostEstimate(
            flops=8 * 2 * rows * D * F, bytes_accessed=6 * D * F + 8 * n_tok * D, transcendentals=rows * F
        ),
    )(ids, route_prob.reshape(1, n_tok), tokens, out_grad, w_gate, w_up, w_down)
    g_tok, g_prob, g_gate, g_up, g_down = pl.pallas_call(
        finish,
        out_shape=(
            jax.ShapeDtypeStruct((n_tok, D), BF),
            jax.ShapeDtypeStruct((1, n_tok), F32),
        )
        + (jax.ShapeDtypeStruct((own, F), BF),) * 3,
        in_specs=[vmem] * 4,
        out_specs=(vmem,) * 5,
    )(ids, packed, psum, g_w)
    return g_tok, g_prob.reshape(n_tok), g_gate, g_up, g_down.T


def solution(mesh):
    placed = (
        P(("dp", "etp"), None),
        P(("dp", "etp"), None),
        P(("dp", "etp"), None),
        P(("dp", "etp")),
        P(None, "etp"),
        P(None, "etp"),
        P("etp", None),
    )
    return jax.shard_map(
        shards,
        mesh=mesh,
        in_specs=placed,
        out_specs=(
            P(("dp", "etp"), None),
            P(("dp", "etp")),
            P("dp", "etp"),
            P("dp", "etp"),
            P("etp", "dp"),
        ),
        check_vma=False,
    )
```

time: 106 us -> 94.6 us (0.89); the launches traced: 106 us -> 93.3 us
  Pallas kernels: 105 us -> 92.7 us
    pallas_call x1, Pallas kernels: 102 us -> 89.9 us  [shards(): pl.pallas_call(kernel, out_shape=(jax.ShapeDtypeStruct((CAP, D), BF), jax...]
where the time goes in v3:
time: 94.6 us; the launch traced here: 93.3 us
  Pallas kernels  92.7 us (98%)
    pallas_call x1, Pallas kernels, shards(): pl.pallas_call(kernel, out_shape=(jax.ShapeDtypeStruct((CAP, D), BF), jax...  89.9 us
    pallas_call x1, Pallas kernels, shards(): pl.pallas_call(finish, out_shape=(jax.ShapeDtypeStruct((n_tok, D), BF), j...  2.77 us

profile of v3, /device:TPU:1, one launch (start us, length us, event | category | flops | bytes accessed | tf_op | source)
XLA Modules:
  0.0 93.3 jit_solution(14959618327985623713)
XLA Ops:
  0.6 89.9 %shard_map.110 = (bf16[32,3072]{1,0:T(8,128)(2,1)}, f32[32,128]{1,0:T(8,128)}, bf16[3,192,512]{2,1,0:T(8,128)(2,1)}) custom-call(s32[2,128]{1,0:T(2,128)} %bitcast.4, bf16[1,128]{1,0:T(2,128)(2,1)} %bitcast.7, bf16[128,3072]{1,0:T(8,128)(2,1)} %tokens_h.1, bf16[128,3072]{1,0:T(8,128)(2,1)} %out_grad_h.1, bf16[3072,512]{1,0:T(8,128)(2,1)} %w_gate_h.1, ...), custom_call_target="tpu_custom_call" | custom-call | flops 12884901888 | bytes 12582912 | tf_op jit(solution)/shard_map/pallas_call | solution.py:672
  90.5 2.8 %shard_map.111 = (bf16[128,3072]{1,0:T(8,128)(2,1)}, f32[1,128]{1,0:T(1,128)}, bf16[192,512]{1,0:T(8,128)(2,1)}, bf16[192,512]{1,0:T(8,128)(2,1)}, bf16[192,512]{1,0:T(8,128)(2,1)}) custom-call(s32[2,128]{1,0:T(2,128)} %bitcast.5, bf16[32,3072]{1,0:T(8,128)(2,1)} %get-tuple-element.13.packed, f32[32,128]{1,0:T(8,128)} %get-tuple-element.14.psum, ...), custom_call_target="tpu_custom_call" | custom-call | tf_op jit(solution)/shard_map/pallas_call | solution.py:689

commit v4 on v3

--- a/solution.py
+++ b/solution.py
@@ -59,7 +59,7 @@
 def kernel(
     ids_h, prob_h, tokens_h, out_grad_h, w_gate_h, w_up_h, w_down_h,
     o_tok, o_prob, o_w,
-    ids, prob, tokens, out_grad, wg, wu, wd, wgt, wut, xs, ds, xt, dt, gs, tp, pb, ws, sr, xa, xb, yb, yc,
+    ids, prob, tokens, out_grad, wg, wu, wd, wgt, wut, xs, ds, xt, dt, gs, tp, pb, ws, wo, sr, xa, xb, yb, yc,
     rp, rph, pr, ry, pry, fw,
     w_sem, o_sem, s_sem, r_sem,
 ):
@@ -93,6 +93,7 @@
     for name in dev:
         pl.semaphore_signal(barrier, inc=1, device_id=dev[name], device_id_type=MESH)
 
+    scope = jax.named_scope
     loads = []
 
     def load(src, dst):
@@ -142,11 +143,6 @@
         ds[0:CAP, D:] = jnp.broadcast_to(w_own, (CAP, 128)).astype(BF)
         loads[2].wait()
         xs[0:CAP, :] = dot(sel_b, tokens[...]).astype(BF)
-        loads[3].wait()
-        ds[0:CAP, 0:D] = dot(sel_b, out_grad[...]).astype(BF)
-        load(w_gate_h, wg)
-        load(w_up_h, wu)
-        load(w_down_h, wd)
 
     with jax.named_scope("barrier_wait"):
         pl.semaphore_wait(barrier, len(dev))
@@ -210,7 +206,7 @@
             r = pair_row(*ORDER[first + q])
             pb[r : r + CAP, :] = pbr[q * CAP : (q + 1) * CAP, :]
 
-    def token_part(first, n, skip=()):
+    def token_part(first, n):
         rows = slice(first * CAP, (first + n) * CAP)
 
         def tok_tile(i, carry):
@@ -220,8 +216,6 @@
                 + dot(gs[1, rows, :], wut[:, pl.ds(at, 512)])
             ).astype(BF)
             for q in range(n):
-                if ORDER[first + q] in skip:
-                    continue
                 r = pair_row(*ORDER[first + q])
                 tp[r : r + CAP, pl.ds(at, 512)] = t[q * CAP : (q + 1) * CAP, :]
             return carry
@@ -355,19 +349,30 @@
         cp.start()
         outs.append(cp)
 
-    def chunk_dot(key, pc, p):
+    early = xs.shape[0] // 2
+
+    def chunk_part(key, pc, p, lo, n):
         dx, h = key
         owner = dp_of((x + dx + 4) % 4, (yh + h) % 2, pc)
         at = pl.multiple_of(owner * rows_own, 64)
         lhs = dt if p == 2 else xt
-        return dot(lhs[pl.ds(at, rows_own), :], gs[p])
+        return dot(lhs[pl.ds(at, rows_own), lo : lo + n], gs[p, lo : lo + n, :])
+
+    def chunk_early(p, keys=CHUNKS):
+        for key in keys:
+            ws[p, CIDX[key]] = chunk_part(key, 1 - core, p, 0, early).astype(BF)
+            wo[p, CIDX[key]] = chunk_part(key, core, p, 0, early).astype(BF)
+
+    def chunk_dot(key, pc, p, first):
+        rest = xs.shape[0] - early
+        return chunk_part(key, pc, p, early, rest) + first[p, CIDX[key]].astype(F32)
 
     from_core = {}
     met = set()
 
     def sib(p, *keys):
         for key in keys:
-            ws[p, CIDX[key]] = chunk_dot(key, 1 - core, p).astype(BF)
+            ws[p, CIDX[key]] = chunk_dot(key, 1 - core, p, ws).astype(BF)
         at = pl.ds(CIDX[keys[0]], len(keys))
         cp = send("c", ws.at[p, at], sr.at[p, at])
         for key in keys:
@@ -376,7 +381,7 @@
     def own(p, *keys):
         for key in keys:
             i = CIDX[key]
-            v = chunk_dot(key, core, p)
+            v = chunk_dot(key, core, p, wo)
             cp = from_core[key, p]
             if id(cp) not in met:
                 met.add(id(cp))
@@ -444,12 +449,17 @@
         fw[p] = (total * (1.0 / 16.0)).astype(BF)
         out(2 + p, fw.at[p], o_w.at[p])
 
-    scope = jax.named_scope
-
     for part in "xd":
+        if part == "d":
+            with scope("pack_d"):
+                loads[3].wait()
+                ds[0:CAP, 0:D] = dot(sel_b, out_grad[...]).astype(BF)
         gsend("z+", (0, 0), (0, 1), part)
         gsend("z-", (0, 0), (0, -1), part)
         ysend(0, part)
+    load(w_gate_h, wg)
+    load(w_up_h, wu)
+    load(w_down_h, wd)
     with scope("wait_weights"):
         for cp in loads[4:]:
             cp.wait()
@@ -488,23 +498,28 @@
     with scope("turn_g1"):
         turn(1, xs, xt)
         turn(1, ds, dt)
+    with scope("early_0"):
+        chunk_early(0)
+        chunk_early(2, CHUNKS[:4])
     with scope("relay_3d"):
         relay(3, "d")
     with scope("wait_g2"):
         gwait((1, 2), (1, -2))
-    with scope("forward_g2"):
-        forward(8, 4)
     with scope("turn_g2"):
         turn(2, xs, xt)
         turn(2, ds, dt)
+    with scope("early_1"):
+        chunk_early(1)
+        chunk_early(2, CHUNKS[4:])
     with scope("relay_4"):
         for part in "xd":
             gwait((0, 4), parts=part)
             ysend(4, part)
     n_gather = len(sent)
-    with scope("far_block"):
-        forward(12, 1)
-        token_part(12, 1)
+    with scope("forward_g2"):
+        forward(8, 5)
+    with scope("token_g2"):
+        token_part(8, 5)
     tok_step(0, 4)
     with scope("wait_g3x"):
         gwait((1, 3), (1, -3), (1, 4), parts="x")
@@ -513,30 +528,30 @@
     with scope("wait_g3d"):
         gwait((1, 3), (1, -3), (1, 4), parts="d")
     with scope("forward_g3"):
-        forward(12, 4)
+        forward(13, 3)
     with scope("drain_gather"):
         drain(n_gather)
     with scope("chunks_a"):
         sib(0, (2, 0), (2, 1))
-    with scope("token_g23"):
-        token_part(8, 8, skip=((0, 4),))
-    tok_step(1, 4)
+    with scope("tok_0_3"):
+        tok_step(0, 3)
+    with scope("turn_d"):
+        turn(3, ds, dt)
+    with scope("chunks_b"):
+        sib(1, (2, 0), (2, 1))
+        sib(2, (2, 1))
+        sib(2, (1, 1))
+        sib(2, (-1, 1))
+        sib(2, (0, 1))
     with scope("far_p0"):
         own(0, (2, 1))
         far_send(1, 0)
         own(0, (2, 0))
         far_send(0, 0)
-    with scope("turn_d"):
-        turn(3, ds, dt)
-    with scope("chunks_b"):
-        sib(2, (2, 1))
-        sib(2, (1, 1))
-        sib(1, (2, 0), (2, 1))
-        sib(2, (-1, 1))
-        sib(2, (0, 1))
-    with scope("tok_0_3"):
-        tok_step(0, 3)
-    with scope("y_first"):
+    with scope("token_g3"):
+        token_part(13, 3)
+    tok_step(1, 4)
+    with scope("y_first_a"):
         own(2, (2, 1))
         y_first(2)
         own(2, (1, 1))
@@ -551,27 +566,27 @@
         y_first(-1)
         own(2, (0, 1))
         y_first(0)
+    with scope("chunks_c"):
+        sib(0, (1, 0), (1, 1), (-1, 0), (-1, 1))
     with scope("tok_1_3"):
         tok_step(1, 3)
-    with scope("chunks_c"):
-        sib(0, (1, 0), (1, 1), (-1, 0), (-1, 1))
+    with scope("near_p0"):
+        own(0, (1, 1), (-1, 1))
+        near_send(1, 0)
+        own(0, (1, 0), (-1, 0))
+        near_send(0, 0)
+    with scope("tok_0_2"):
+        tok_step(0, 2)
+    with scope("chunks_d"):
         sib(1, (1, 0), (1, 1), (-1, 0), (-1, 1))
-        own(0, (1, 1), (-1, 1), (1, 0), (-1, 0))
-    with scope("near_p0"):
-        near_send(1, 0)
-        near_send(0, 0)
-    with scope("chunks_d"):
         sib(2, (2, 0))
         sib(2, (1, 0))
         sib(2, (-1, 0))
-    with scope("tok_0_2"):
-        tok_step(0, 2)
+        own(1, (1, 1), (-1, 1), (1, 0), (-1, 0))
+        own(2, (2, 0))
     with scope("y_add_2"):
-        own(2, (2, 0))
         y_add(2)
         far_send(0, 2)
-    with scope("chunks_e"):
-        own(1, (1, 1), (-1, 1), (1, 0), (-1, 0))
     with scope("near_p1"):
         near_send(1, 1)
         near_send(0, 1)
@@ -586,11 +601,12 @@
         own(0, (0, 1), (0, 0))
         own(1, (0, 1), (0, 0))
         own(2, (0, 0))
-    with scope("y_add_near"):
+    with scope("y_add_1"):
         y_add(1)
-        y_add(-1)
     with scope("y_last_0"):
         y_last(0)
+    with scope("y_add_m1"):
+        y_add(-1)
     with scope("tok_1_1"):
         tok_step(1, 1)
     with scope("tok_0_1"):
@@ -599,18 +615,18 @@
         near_send(0, 2)
     with scope("y_add_0"):
         y_add(0)
-    with scope("tok_cross"):
-        crossing = tok_cross()
     with scope("y_last_1"):
         y_last(1)
     with scope("w_final_0"):
         w_final(0)
+    with scope("tok_cross"):
+        crossing = tok_cross()
     with scope("tok_final"):
         tok_final(crossing)
+    with scope("w_final_1"):
+        w_final(1)
     with scope("w_final_2"):
         w_final(2)
-    with scope("w_final_1"):
-        w_final(1)
     with scope("drain"):
         drain(len(sent))
         for cp in outs:
@@ -651,6 +667,7 @@
         pltpu.VMEM((3, rows, F), BF),
         pltpu.VMEM((rows, D), BF),
         pltpu.VMEM((rows, 128), F32),
+        pltpu.VMEM((3, 8, own, F), BF),
         pltpu.VMEM((3, 8, own, F), BF),
         pltpu.VMEM((3, 8, own, F), BF),
         pltpu.VMEM((2, 3, own, F), BF),

time: 94.6 us -> 92.9 us (0.982); the launches traced: 93.3 us -> 92.7 us
  no operation moved by 1% of the time
where the time goes in v4:
time: 92.9 us; the launch traced here: 92.7 us
  Pallas kernels  92.1 us (99%)
    pallas_call x1, Pallas kernels, shards(): pl.pallas_call(kernel, out_shape=(jax.ShapeDtypeStruct((CAP, D), BF), jax...  89.3 us
    pallas_call x1, Pallas kernels, shards(): pl.pallas_call(finish, out_shape=(jax.ShapeDtypeStruct((n_tok, D), BF), j...  2.77 us

profile of v4, /device:TPU:1, one launch (start us, length us, event | category | flops | bytes accessed | tf_op | source)
XLA Modules:
  0.0 92.7 jit_solution(10790185266368603438)
XLA Ops:
  0.6 89.3 %shard_map.110 = (bf16[32,3072]{1,0:T(8,128)(2,1)}, f32[32,128]{1,0:T(8,128)}, bf16[3,192,512]{2,1,0:T(8,128)(2,1)}) custom-call(s32[2,128]{1,0:T(2,128)} %bitcast.4, bf16[1,128]{1,0:T(2,128)(2,1)} %bitcast.7, bf16[128,3072]{1,0:T(8,128)(2,1)} %tokens_h.1, bf16[128,3072]{1,0:T(8,128)(2,1)} %out_grad_h.1, bf16[3072,512]{1,0:T(8,128)(2,1)} %w_gate_h.1, ...), custom_call_target="tpu_custom_call" | custom-call | flops 12884901888 | bytes 12582912 | tf_op jit(solution)/shard_map/pallas_call | solution.py:689
  90.0 2.8 %shard_map.111 = (bf16[128,3072]{1,0:T(8,128)(2,1)}, f32[1,128]{1,0:T(1,128)}, bf16[192,512]{1,0:T(8,128)(2,1)}, bf16[192,512]{1,0:T(8,128)(2,1)}, bf16[192,512]{1,0:T(8,128)(2,1)}) custom-call(s32[2,128]{1,0:T(2,128)} %bitcast.5, bf16[32,3072]{1,0:T(8,128)(2,1)} %get-tuple-element.13.packed, f32[32,128]{1,0:T(8,128)} %get-tuple-element.14.psum, ...), custom_call_target="tpu_custom_call" | custom-call | tf_op jit(solution)/shard_map/pallas_call | solution.py:706

commit v5 on v4

--- a/solution.py
+++ b/solution.py
@@ -34,6 +34,11 @@
 
 def dot_t(a, b):
     return lax.dot_general(a, b, (((1,), (1,)), ((), ())), preferred_element_type=F32)
+
+
+def diagonal():
+    shape = (CAP, 128)
+    return lax.broadcasted_iota(jnp.int32, shape, 0) == lax.broadcasted_iota(jnp.int32, shape, 1)
 
 
 def routed_rows(ids):
@@ -60,7 +65,7 @@
     ids_h, prob_h, tokens_h, out_grad_h, w_gate_h, w_up_h, w_down_h,
     o_tok, o_prob, o_w,
     ids, prob, tokens, out_grad, wg, wu, wd, wgt, wut, xs, ds, xt, dt, gs, tp, pb, ws, wo, sr, xa, xb, yb, yc,
-    rp, rph, pr, ry, pry, fw,
+    rp, rph, pr, ry, pry, fp, fw,
     w_sem, o_sem, s_sem, r_sem,
 ):
     D = xs.shape[1]
@@ -107,32 +112,26 @@
     load(out_grad_h, out_grad)
 
     count = [0]
-    sent, free = [], list(range(s_sem.shape[0]))
-
-    def drain(n):
-        for cp, k in sent[:n]:
-            cp.wait_send()
-            free.append(k)
-        del sent[:n]
-
-    def send(name, src, dst):
-        return send_all([(name, src, dst)], src, dst)
-
-    def send_all(items, src, dst):
-        i, k = count[0], free.pop(0)
+    groups = {"x": 0, "d": 1, "core": 2, "weight": 3, "token": 4, "prob": 5}
+
+    def remote(group, i, name, src, dst):
+        return pltpu.make_async_remote_copy(
+            src_ref=src, dst_ref=dst, send_sem=s_sem.at[groups[group]], recv_sem=r_sem.at[i],
+            device_id=dev[name], device_id_type=MESH,
+        )
+
+    def send(group, name, src, dst):
+        return send_all(group, [(name, src, dst)], src, dst)
+
+    def send_all(group, items, src, dst):
+        i = count[0]
         count[0] += 1
-
-        def copy(name, a, b):
-            return pltpu.make_async_remote_copy(
-                src_ref=a, dst_ref=b, send_sem=s_sem.at[k], recv_sem=r_sem.at[i],
-                device_id=dev[name], device_id_type=MESH,
-            )
-
-        for item in items:
-            copy(*item).start()
-        whole = copy(items[0][0], src, dst)
-        sent.append((whole, k))
-        return whole
+        for name, a, b in items:
+            remote(group, i, name, a, b).start()
+        return remote(group, i, items[0][0], src, dst)
+
+    def drain(group, ref):
+        remote(group, 0, "c", ref, ref).wait_send()
 
     with jax.named_scope("pack"):
         loads[0].wait()
@@ -152,12 +151,13 @@
     def gsend(name, key, to, part):
         a, b = pl.ds(SLOT[key] * CAP, CAP), pl.ds(SLOT[to] * CAP, CAP)
         buf = xs if part == "x" else ds
-        arriving[to + (part,)] = send(name, buf.at[a, :], buf.at[b, :])
+        arriving[to + (part,)] = send(part, name, buf.at[a, :], buf.at[b, :])
 
     def ysend(off, part):
         buf = xs if part == "x" else ds
         a, b = SLOT[(0, off)] * CAP, SLOT[(1, off)] * CAP
         arriving[(1, off, part)] = send_all(
+            part,
             [
                 (name, buf.at[pl.ds(a + q * HALF, HALF), :], buf.at[pl.ds(b + q * HALF, HALF), :])
                 for q, name in ((0, "y+"), (1, "y-"))
@@ -203,8 +203,11 @@
             psum = psum + jnp.sum(hid * raw, axis=1, keepdims=True)
         pbr = jnp.broadcast_to(psum, (m, 128))
         for q in range(n):
-            r = pair_row(*ORDER[first + q])
-            pb[r : r + CAP, :] = pbr[q * CAP : (q + 1) * CAP, :]
+            c, off = ORDER[first + q]
+            row = jnp.sum(
+                jnp.where(diagonal(), pbr[q * CAP : (q + 1) * CAP, :], 0.0), axis=0, keepdims=True
+            )
+            pb[off % 8, c] = jnp.broadcast_to(row, (8, 128))
 
     def token_part(first, n):
         rows = slice(first * CAP, (first + n) * CAP)
@@ -246,13 +249,13 @@
     def tok_step(c, k):
         sides = ((0, "z+", -1), (1, "z-", 1))
         rows = [pair_row(c, sign * k) for _, _, sign in sides]
-        pairs = [pair_row(0, sign * k) for _, _, sign in sides]
-        pair = 2 * CAP
+        offs = [sign * k % 8 for _, _, sign in sides]
         if k < 4:
             before_t, before_p = chain[c, k + 1]
             before_t.wait_recv()
         if k == 4:
             got = send_all(
+                "token",
                 [
                     (name, tp.at[pl.ds(rows[i], CAP), slice(i * H, (i + 1) * H)], rph.at[i, c])
                     for i, name, _ in sides
@@ -267,6 +270,7 @@
                 else:
                     add_rows(tp, rows[i], rp.at[c, 2 - k, i], CAP, slice(0, D))
             got = send_all(
+                "token",
                 [(name, tp.at[pl.ds(rows[i], CAP), :], rp.at[c, 3 - k, i]) for i, name, _ in sides],
                 rp.at[c, 3 - k],
                 rp.at[c, 3 - k],
@@ -274,17 +278,14 @@
         gotp = None
         if c == 1:
             if k == 4:
-                gotp = send("z+", pb.at[pl.ds(pairs[0], pair), :], pr.at[0, 0])
+                gotp = send("prob", "z+", pb.at[4], pr.at[0, 0])
             else:
                 before_p.wait_recv()
                 for i in (0, 1) if k < 3 else (0,):
-                    both = slice(pairs[i], pairs[i] + pair)
-                    pb[both, :] = pb[both, :] + pr[3 - k, i]
+                    pb[offs[i]] = pb[offs[i]] + pr[3 - k, i]
                 gotp = send_all(
-                    [
-                        (name, pb.at[pl.ds(pairs[i], pair), :], pr.at[4 - k, i])
-                        for i, name, _ in sides
-                    ],
+                    "prob",
+                    [(name, pb.at[offs[i]], pr.at[4 - k, i]) for i, name, _ in sides],
                     pr.at[4 - k],
                     pr.at[4 - k],
                 )
@@ -294,8 +295,6 @@
         for cp in chain[c, 1]:
             if cp is not None:
                 cp.wait_recv()
-
-    own_rows, other_rows = slice(0, CAP), slice(CAP, 2 * CAP)
 
     def tok_cross():
         tok_arrived(1)
@@ -309,20 +308,20 @@
             return carry
 
         lax.fori_loop(0, CAP // 16, body, 0)
-        pb[other_rows, :] = pb[other_rows, :] + pr[3, 0, other_rows] + pr[3, 1, other_rows]
-        crossing = []
-        for src, dst in ((tp, ry), (pb, pry)):
-            crossing.append(
-                send_all(
-                    [
-                        (name, src.at[pl.ds(CAP + q * HALF, HALF), :], dst.at[pl.ds(q * HALF, HALF), :])
-                        for q, name in ((0, "y-"), (1, "y+"))
-                    ],
-                    src.at[pl.ds(CAP, CAP), :],
-                    dst,
-                )
-            )
-        return crossing
+        pb[0, 1] = pb[0, 1] + pr[3, 0, 1] + pr[3, 1, 1]
+        sides = ((0, "y-"), (1, "y+"))
+        return (
+            send_all(
+                "token",
+                [
+                    (name, tp.at[pl.ds(CAP + q * HALF, HALF), :], ry.at[pl.ds(q * HALF, HALF), :])
+                    for q, name in sides
+                ],
+                tp.at[pl.ds(CAP, CAP), :],
+                ry,
+            ),
+            send_all("prob", [(name, pb.at[0, 1], pry.at[q]) for q, name in sides], pry, pry),
+        )
 
     def tok_final(crossing):
         tok_arrived(0)
@@ -338,9 +337,10 @@
             return carry
 
         lax.fori_loop(0, CAP // 16, body, 0)
-        pry[...] = pb[own_rows, :] + pr[3, 0, own_rows] + pr[3, 1, own_rows] + pry[...]
+        lane = lax.broadcasted_iota(jnp.int32, (8, 128), 1)
+        fp[...] = pb[0, 0] + pr[3, 0, 0] + pr[3, 1, 0] + jnp.where(lane < HALF, pry[0], pry[1])
         out(0, ry, o_tok)
-        out(1, pry, o_prob)
+        out(1, fp, o_prob)
 
     outs = []
 
@@ -374,7 +374,7 @@
         for key in keys:
             ws[p, CIDX[key]] = chunk_dot(key, 1 - core, p, ws).astype(BF)
         at = pl.ds(CIDX[keys[0]], len(keys))
-        cp = send("c", ws.at[p, at], sr.at[p, at])
+        cp = send("core", "c", ws.at[p, at], sr.at[p, at])
         for key in keys:
             from_core[key, p] = cp
 
@@ -393,6 +393,7 @@
     def far_send(h, p):
         i = CIDX[(2, h)]
         far[h, p] = send_all(
+            "weight",
             [
                 (name, sr.at[p, i, pl.ds(q * half, half), :], xa.at[h, p, pl.ds(q * half, half), :])
                 for q, name in ((0, "x+"), (1, "x-"))
@@ -410,6 +411,7 @@
             r = slice(q * half, (q + 1) * half)
             sr[p, i, r, :] = (sr[p, i, r, :].astype(F32) + xa[h, p, r, :].astype(F32)).astype(BF)
         near[h, p] = send_all(
+            "weight",
             [
                 (name, sr.at[p, CIDX[(dx, h)]], xb.at[h, p, q])
                 for q, name, dx in ((0, "x+", 1), (1, "x-", -1))
@@ -429,10 +431,10 @@
         sr[p, i] = (
             sr[p, i].astype(F32) + xb[1, p, 0].astype(F32) + xb[1, p, 1].astype(F32)
         ).astype(BF)
-        to_y[p] = send("y2", sr.at[p, i], yb.at[p])
+        to_y[p] = send("weight", "y2", sr.at[p, i], yb.at[p])
 
     def y_first(dx):
-        to_y[2, dx] = send("y2", sr.at[2, CIDX[(dx, 1)]], yc.at[CIDX[(dx, 0)] // 2])
+        to_y[2, dx] = send("weight", "y2", sr.at[2, CIDX[(dx, 1)]], yc.at[CIDX[(dx, 0)] // 2])
 
     def y_add(dx):
         to_y[2, dx].wait_recv()
@@ -515,7 +517,6 @@
         for part in "xd":
             gwait((0, 4), parts=part)
             ysend(4, part)
-    n_gather = len(sent)
     with scope("forward_g2"):
         forward(8, 5)
     with scope("token_g2"):
@@ -529,8 +530,6 @@
         gwait((1, 3), (1, -3), (1, 4), parts="d")
     with scope("forward_g3"):
         forward(13, 3)
-    with scope("drain_gather"):
-        drain(n_gather)
     with scope("chunks_a"):
         sib(0, (2, 0), (2, 1))
     with scope("tok_0_3"):
@@ -541,21 +540,21 @@
         sib(1, (2, 0), (2, 1))
         sib(2, (2, 1))
         sib(2, (1, 1))
-        sib(2, (-1, 1))
-        sib(2, (0, 1))
     with scope("far_p0"):
         own(0, (2, 1))
         far_send(1, 0)
         own(0, (2, 0))
         far_send(0, 0)
-    with scope("token_g3"):
-        token_part(13, 3)
-    tok_step(1, 4)
     with scope("y_first_a"):
         own(2, (2, 1))
         y_first(2)
         own(2, (1, 1))
         y_first(1)
+    with scope("token_g3"):
+        sib(2, (-1, 1))
+        sib(2, (0, 1))
+        token_part(13, 3)
+    tok_step(1, 4)
     with scope("far_p1"):
         own(1, (2, 1))
         far_send(1, 1)
@@ -568,27 +567,29 @@
         y_first(0)
     with scope("chunks_c"):
         sib(0, (1, 0), (1, 1), (-1, 0), (-1, 1))
+        sib(1, (1, 0), (1, 1), (-1, 0), (-1, 1))
     with scope("tok_1_3"):
         tok_step(1, 3)
     with scope("near_p0"):
         own(0, (1, 1), (-1, 1))
         near_send(1, 0)
-        own(0, (1, 0), (-1, 0))
-        near_send(0, 0)
+        own(1, (1, 1), (-1, 1))
     with scope("tok_0_2"):
         tok_step(0, 2)
     with scope("chunks_d"):
-        sib(1, (1, 0), (1, 1), (-1, 0), (-1, 1))
         sib(2, (2, 0))
         sib(2, (1, 0))
         sib(2, (-1, 0))
-        own(1, (1, 1), (-1, 1), (1, 0), (-1, 0))
+        own(0, (1, 0), (-1, 0))
+        own(1, (1, 0), (-1, 0))
         own(2, (2, 0))
+    with scope("near_p1"):
+        near_send(1, 1)
     with scope("y_add_2"):
         y_add(2)
         far_send(0, 2)
-    with scope("near_p1"):
-        near_send(1, 1)
+    with scope("near_h0"):
+        near_send(0, 0)
         near_send(0, 1)
     with scope("chunks_f"):
         sib(0, (0, 0), (0, 1))
@@ -617,10 +618,10 @@
         y_add(0)
     with scope("y_last_1"):
         y_last(1)
+    with scope("tok_cross"):
+        crossing = tok_cross()
     with scope("w_final_0"):
         w_final(0)
-    with scope("tok_cross"):
-        crossing = tok_cross()
     with scope("tok_final"):
         tok_final(crossing)
     with scope("w_final_1"):
@@ -628,7 +629,12 @@
     with scope("w_final_2"):
         w_final(2)
     with scope("drain"):
-        drain(len(sent))
+        drain("x", xs.at[pl.ds(0, 15 * CAP)])
+        drain("d", ds.at[pl.ds(0, 15 * CAP)])
+        drain("core", ws)
+        drain("weight", sr.at[:, pl.ds(0, 7)])
+        drain("token", tp.at[pl.ds(0, 15 * CAP)])
+        drain("prob", pb)
         for cp in outs:
             cp.wait()
 
@@ -639,7 +645,10 @@
     o_up[...] = w_in[1]
     o_down[...] = w_in[2]
     o_tok[...] = dot(sel.T.astype(BF), packed[...]).astype(BF)
-    o_prob[...] = jnp.sum(sel * psum[...], axis=0, keepdims=True)
+    prob = jnp.sum(
+        jnp.where(diagonal(), jnp.broadcast_to(psum[0:1, :], (CAP, 128)), 0.0), axis=1, keepdims=True
+    )
+    o_prob[...] = jnp.sum(sel * prob, axis=0, keepdims=True)
 
 
 def shards(tokens, out_grad, route_ids, route_prob, w_gate, w_up, w_down):
@@ -649,7 +658,7 @@
     rows = CAP * lax.axis_size("etp")
     vmem = pl.BlockSpec(memory_space=pltpu.VMEM)
     hbm = pl.BlockSpec(memory_space=pl.ANY)
-    n_send, n_recv = 45, 74
+    n_send, n_recv = 6, 74
     scratch = [
         pltpu.VMEM((2, n_tok), jnp.int32),
         pltpu.VMEM((1, n_tok), BF),
@@ -666,7 +675,7 @@
         pltpu.VMEM((D, rows), BF),
         pltpu.VMEM((3, rows, F), BF),
         pltpu.VMEM((rows, D), BF),
-        pltpu.VMEM((rows, 128), F32),
+        pltpu.VMEM((8, 2, 8, 128), F32),
         pltpu.VMEM((3, 8, own, F), BF),
         pltpu.VMEM((3, 8, own, F), BF),
         pltpu.VMEM((3, 8, own, F), BF),
@@ -676,9 +685,10 @@
         pltpu.VMEM((4, own, F), BF),
         pltpu.VMEM((2, 3, 2, CAP, D), BF),
         pltpu.VMEM((2, 2, CAP, D // 2), BF),
-        pltpu.VMEM((4, 2, 2 * CAP, 128), F32),
+        pltpu.VMEM((4, 2, 2, 8, 128), F32),
         pltpu.VMEM((CAP, D), BF),
-        pltpu.VMEM((CAP, 128), F32),
+        pltpu.VMEM((2, 8, 128), F32),
+        pltpu.VMEM((8, 128), F32),
         pltpu.VMEM((3, own, F), BF),
         pltpu.SemaphoreType.DMA((7,)),
         pltpu.SemaphoreType.DMA((5,)),
@@ -690,7 +700,7 @@
         kernel,
         out_shape=(
             jax.ShapeDtypeStruct((CAP, D), BF),
-            jax.ShapeDtypeStruct((CAP, 128), F32),
+            jax.ShapeDtypeStruct((8, 128), F32),
             jax.ShapeDtypeStruct((3, own, F), BF),
         ),
         in_specs=[hbm] * 7,

time: 92.9 us -> 94.4 us (1.016)
    pallas_call x1, Pallas kernels: 89.3 us -> 90.3 us  [shards(): pl.pallas_call(kernel, out_shape=(jax.ShapeDtypeStruct((CAP, D), BF), jax...]
where the time goes in v5:
time: 94.4 us; the launch traced here: 93.7 us
  Pallas kernels  93 us (99%)
    pallas_call x1, Pallas kernels, shards(): pl.pallas_call(kernel, out_shape=(jax.ShapeDtypeStruct((CAP, D), BF), jax...  90.3 us
    pallas_call x1, Pallas kernels, shards(): pl.pallas_call(finish, out_shape=(jax.ShapeDtypeStruct((n_tok, D), BF), j...  2.75 us

profile of v5, /device:TPU:1, one launch (start us, length us, event | category | flops | bytes accessed | tf_op | source)
XLA Modules:
  0.0 93.7 jit_solution(2212731950201090284)
XLA Ops:
  0.6 90.3 %shard_map.110 = (bf16[32,3072]{1,0:T(8,128)(2,1)}, f32[8,128]{1,0:T(8,128)}, bf16[3,192,512]{2,1,0:T(8,128)(2,1)}) custom-call(s32[2,128]{1,0:T(2,128)} %bitcast.4, bf16[1,128]{1,0:T(2,128)(2,1)} %bitcast.7, bf16[128,3072]{1,0:T(8,128)(2,1)} %tokens_h.1, bf16[128,3072]{1,0:T(8,128)(2,1)} %out_grad_h.1, bf16[3072,512]{1,0:T(8,128)(2,1)} %w_gate_h.1, ...), custom_call_target="tpu_custom_call" | custom-call | flops 12884901888 | bytes 12582912 | tf_op jit(solution)/shard_map/pallas_call | solution.py:699
  90.9 2.8 %shard_map.111 = (bf16[128,3072]{1,0:T(8,128)(2,1)}, f32[1,128]{1,0:T(1,128)}, bf16[192,512]{1,0:T(8,128)(2,1)}, bf16[192,512]{1,0:T(8,128)(2,1)}, bf16[192,512]{1,0:T(8,128)(2,1)}) custom-call(s32[2,128]{1,0:T(2,128)} %bitcast.5, bf16[32,3072]{1,0:T(8,128)(2,1)} %get-tuple-element.13.packed, f32[8,128]{1,0:T(8,128)} %get-tuple-element.14.psum, ...), custom_call_target="tpu_custom_call" | custom-call | tf_op jit(solution)/shard_map/pallas_call | solution.py:716

commit v6 on v5

--- a/solution.py
+++ b/solution.py
@@ -545,16 +545,16 @@
         far_send(1, 0)
         own(0, (2, 0))
         far_send(0, 0)
+    with scope("token_g3"):
+        sib(2, (-1, 1))
+        sib(2, (0, 1))
+        token_part(13, 3)
+    tok_step(1, 4)
     with scope("y_first_a"):
         own(2, (2, 1))
         y_first(2)
         own(2, (1, 1))
         y_first(1)
-    with scope("token_g3"):
-        sib(2, (-1, 1))
-        sib(2, (0, 1))
-        token_part(13, 3)
-    tok_step(1, 4)
     with scope("far_p1"):
         own(1, (2, 1))
         far_send(1, 1)

time: 94.4 us -> 92.7 us (0.982)
  Pallas kernels: 93 us -> 91.9 us
    pallas_call x1, Pallas kernels: 90.3 us -> 89.1 us  [shards(): pl.pallas_call(kernel, out_shape=(jax.ShapeDtypeStruct((CAP, D), BF), jax...]
where the time goes in v6:
time: 92.7 us; the launch traced here: 92.5 us
  Pallas kernels  91.9 us (99%)
    pallas_call x1, Pallas kernels, shards(): pl.pallas_call(kernel, out_shape=(jax.ShapeDtypeStruct((CAP, D), BF), jax...  89.1 us
    pallas_call x1, Pallas kernels, shards(): pl.pallas_call(finish, out_shape=(jax.ShapeDtypeStruct((n_tok, D), BF), j...  2.75 us

profile of v6, /device:TPU:1, one launch (start us, length us, event | category | flops | bytes accessed | tf_op | source)
XLA Modules:
  0.0 92.5 jit_solution(12935873844214571095)
XLA Ops:
  0.6 89.1 %shard_map.110 = (bf16[32,3072]{1,0:T(8,128)(2,1)}, f32[8,128]{1,0:T(8,128)}, bf16[3,192,512]{2,1,0:T(8,128)(2,1)}) custom-call(s32[2,128]{1,0:T(2,128)} %bitcast.4, bf16[1,128]{1,0:T(2,128)(2,1)} %bitcast.7, bf16[128,3072]{1,0:T(8,128)(2,1)} %tokens_h.1, bf16[128,3072]{1,0:T(8,128)(2,1)} %out_grad_h.1, bf16[3072,512]{1,0:T(8,128)(2,1)} %w_gate_h.1, ...), custom_call_target="tpu_custom_call" | custom-call | flops 12884901888 | bytes 12582912 | tf_op jit(solution)/shard_map/pallas_call | solution.py:699
  89.8 2.8 %shard_map.111 = (bf16[128,3072]{1,0:T(8,128)(2,1)}, f32[1,128]{1,0:T(1,128)}, bf16[192,512]{1,0:T(8,128)(2,1)}, bf16[192,512]{1,0:T(8,128)(2,1)}, bf16[192,512]{1,0:T(8,128)(2,1)}) custom-call(s32[2,128]{1,0:T(2,128)} %bitcast.5, bf16[32,3072]{1,0:T(8,128)(2,1)} %get-tuple-element.13.packed, f32[8,128]{1,0:T(8,128)} %get-tuple-element.14.psum, ...), custom_call_target="tpu_custom_call" | custom-call | tf_op jit(solution)/shard_map/pallas_call | solution.py:716

commit v7 on v6

--- a/solution.py
+++ b/solution.py
@@ -531,21 +531,22 @@
     with scope("forward_g3"):
         forward(13, 3)
     with scope("chunks_a"):
-        sib(0, (2, 0), (2, 1))
+        sib(0, (2, 1))
+        sib(0, (2, 0))
     with scope("tok_0_3"):
         tok_step(0, 3)
     with scope("turn_d"):
         turn(3, ds, dt)
     with scope("chunks_b"):
         sib(1, (2, 0), (2, 1))
-        sib(2, (2, 1))
-        sib(2, (1, 1))
     with scope("far_p0"):
         own(0, (2, 1))
         far_send(1, 0)
         own(0, (2, 0))
         far_send(0, 0)
     with scope("token_g3"):
+        sib(2, (2, 1))
+        sib(2, (1, 1))
         sib(2, (-1, 1))
         sib(2, (0, 1))
         token_part(13, 3)
@@ -658,7 +659,7 @@
     rows = CAP * lax.axis_size("etp")
     vmem = pl.BlockSpec(memory_space=pltpu.VMEM)
     hbm = pl.BlockSpec(memory_space=pl.ANY)
-    n_send, n_recv = 6, 74
+    n_send, n_recv = 6, 75
     scratch = [
         pltpu.VMEM((2, n_tok), jnp.int32),
         pltpu.VMEM((1, n_tok), BF),

time: 92.7 us -> 92.6 us (level)
  no operation moved by 1% of the time
where the time goes in v7:
time: 92.6 us; the launch traced here: 92.5 us
  Pallas kernels  91.8 us (99%)
    pallas_call x1, Pallas kernels, shards(): pl.pallas_call(kernel, out_shape=(jax.ShapeDtypeStruct((CAP, D), BF), jax...  89.1 us
    pallas_call x1, Pallas kernels, shards(): pl.pallas_call(finish, out_shape=(jax.ShapeDtypeStruct((n_tok, D), BF), j...  2.76 us

profile of v7, /device:TPU:1, one launch (start us, length us, event | category | flops | bytes accessed | tf_op | source)
XLA Modules:
  0.0 92.5 jit_solution(2582455869198134625)
XLA Ops:
  0.6 89.1 %shard_map.110 = (bf16[32,3072]{1,0:T(8,128)(2,1)}, f32[8,128]{1,0:T(8,128)}, bf16[3,192,512]{2,1,0:T(8,128)(2,1)}) custom-call(s32[2,128]{1,0:T(2,128)} %bitcast.4, bf16[1,128]{1,0:T(2,128)(2,1)} %bitcast.7, bf16[128,3072]{1,0:T(8,128)(2,1)} %tokens_h.1, bf16[128,3072]{1,0:T(8,128)(2,1)} %out_grad_h.1, bf16[3072,512]{1,0:T(8,128)(2,1)} %w_gate_h.1, ...), custom_call_target="tpu_custom_call" | custom-call | flops 12884901888 | bytes 12582912 | tf_op jit(solution)/shard_map/pallas_call | solution.py:700
  89.7 2.8 %shard_map.111 = (bf16[128,3072]{1,0:T(8,128)(2,1)}, f32[1,128]{1,0:T(1,128)}, bf16[192,512]{1,0:T(8,128)(2,1)}, bf16[192,512]{1,0:T(8,128)(2,1)}, bf16[192,512]{1,0:T(8,128)(2,1)}) custom-call(s32[2,128]{1,0:T(2,128)} %bitcast.5, bf16[32,3072]{1,0:T(8,128)(2,1)} %get-tuple-element.13.packed, f32[8,128]{1,0:T(8,128)} %get-tuple-element.14.psum, ...), custom_call_target="tpu_custom_call" | custom-call | tf_op jit(solution)/shard_map/pallas_call | solution.py:717
